TPU v7x, 1024 devices: a whole 4x4x32 slice. The times are simulated.
1024 devices in a mesh: tower: 8 (over x, core), inner: 128 (over z, y).
Axes of the slice: x: 4, y: 4, z: 32, core: 2. Of those that a mesh axis runs over, the one named last changes fastest.
Arguments:
- grad_inter: bfloat16 [128, 16, 8192], P('inner', 'tower'), may hold values from -6 to 6
- pooled: bfloat16 [8, 2048, 16384], P('tower', None, 'inner'), may hold values from -6 to 6
- tower_weight: bfloat16 [8, 16384, 1024], P('tower', 'inner'), may hold values from -0.1875 to 0.1875
- indices: int32 [8, 128, 2048, 16], P('tower', 'inner'), may hold values from 0 to 1023
- lengths: int32 [8, 128, 2048], P('tower', 'inner'), may hold values from 1 to 16, as said below
- table_slab: float32 [8, 131072, 128], P('tower', 'inner'), may hold values from -0.3 to 0.3
- accumulator: float32 [8, 131072, 128], P('tower', 'inner'), may hold values from 0.1 to 1
Outputs:
- weight_grad: float32 [8, 16384, 1024], P('tower', 'inner')
- new_table: float32 [8, 131072, 128], P('tower', 'inner')
- new_accum: float32 [8, 131072, 128], P('tower', 'inner')
Inputs may be any that keep to these rules, and one draw needn't show every extreme that they name: Only the first lengths entries of a bag are live; every device holds some bag of length 16.
All inputs are finite; a program needn't handle non-finite values.
Results may differ from a plain program's by a relative error of at most 0.0051.
Values may be sent and summed in bfloat16 or wider, within the bound.
No kernel may reach another device: no remote copies, remote signals or barrier semaphores. Data moves between devices by JAX's collectives and lax.ppermute only.
A program may use at most 32 MiB of HBM per device.

v0:
```python
import jax
import jax.numpy as jnp
from jax import lax
from jax.sharding import PartitionSpec as P

learn_rate = 0.1
epsilon = 1e-08


def per_device(grad_inter, pooled, tower_weight, indices, lengths, table_slab, accumulator):
    received = lax.all_to_all(grad_inter, "tower", split_axis=2, concat_axis=1, tiled=True)
    width = received.shape[2]
    feats = pooled[0]
    weights = tower_weight[0]
    samples = feats.shape[0]
    emb_width = feats.shape[1]
    gathered = lax.all_gather(received, "inner", axis=0, tiled=True).reshape(-1, width)
    wgrad = lax.dot_general(
        feats, gathered, (((0,), (0,)), ((), ())), preferred_element_type=jnp.float32
    )
    pgrad = lax.dot_general(
        gathered, weights, (((1,), (1,)), ((), ())), preferred_element_type=jnp.float32
    ).astype(jnp.bfloat16)
    index_rows = indices[0, 0]
    bag_lengths = lengths[0, 0]
    slab = table_slab[0]
    sums = accumulator[0]
    slab_rows = slab.shape[0]
    bag_size = index_rows.shape[1]
    block_rows = min(256, samples)
    row_ids = jnp.arange(slab_rows, dtype=jnp.int32)

    def accumulate(step_index, totals):
        low_row = step_index * block_rows
        index_block = lax.dynamic_slice_in_dim(index_rows, low_row, block_rows, 0)
        length_block = lax.dynamic_slice_in_dim(bag_lengths, low_row, block_rows, 0)
        grad_block = lax.dynamic_slice_in_dim(pgrad, low_row, block_rows, 0)
        live = jnp.arange(bag_size)[None, :] < length_block[:, None]
        hits = (index_block[:, :, None] == row_ids[None, None, :]) & live[:, :, None]
        counts = jnp.sum(hits, axis=1, dtype=jnp.float32).astype(jnp.bfloat16)
        return totals + lax.dot_general(
            counts, grad_block, (((0,), (0,)), ((), ())), preferred_element_type=jnp.float32
        )

    row_grad = lax.fori_loop(
        0, samples // block_rows, accumulate, jnp.zeros((slab_rows, emb_width), jnp.float32)
    )
    fresh = sums + row_grad * row_grad
    updated = slab - learn_rate * row_grad / (jnp.sqrt(fresh) + epsilon)
    return (wgrad[None], updated[None], fresh[None])


def solution(mesh):
    return jax.shard_map(
        per_device,
        mesh=mesh,
        in_specs=(
            P("inner", "tower", None),
            P("tower", None, "inner"),
            P("tower", "inner", None),
            P("tower", "inner", None, None),
            P("tower", "inner", None),
            P("tower", "inner", None),
            P("tower", "inner", None),
        ),
        out_specs=(P("tower", "inner", None), P("tower", "inner", None), P("tower", "inner", None)),
        check_vma=False,
    )
```

profile of v0, /device:TPU:6, one launch (start us, length us, event | category | flops | bytes accessed | tf_op | source)
XLA Modules:
  0.0 440.1 jit_solution(16141995438441525906)
XLA Ops:
  7.2 8.3 %copy.20 = bf16[1,2,8192]{1,0,2:T(2,128)(2,1)} copy(bf16[1,2,8192]{2,1,0:T(2,128)(2,1)} %param.9) | data formatting | bytes 65536 | tf_op args[0]
  16.0 45.2 %reduce = bf16[8192,2]{1,0:T(8,128)(2,1)S(1)} reduce(bf16[8192,1,2]{2,1,0:T(2,128)(2,1)} %bitcast.41, bf16[]{:T(256)} %broadcast.24), dimensions={1}, to_apply=%bitcast.32.reduce_sub_computation | reduce | bytes 65538
  61.3 3.2 reshape.33
  64.5 18.9 %all_to_all.18 = bf16[8,2,1024]{2,1,0:T(2,128)(2,1)S(1)} all-to-all(bf16[8,2,1024]{2,1,0:T(2,128)(2,1)S(1)} %reshape.33), channel_id=1, replica_groups=mesh['tower'=8,'inner'=128] {'tower'}, dimensions={0} | all-to-all | bytes 65536 | tf_op jit(solution)/shard_map/all_to_all | solution.py:11
  83.4 6.2 %reshape.34 = bf16[8192,1,2]{2,1,0:T(2,128)(2,1)} reshape(bf16[8,2,1024]{2,1,0:T(2,128)(2,1)S(1)} %all_to_all.18) | data formatting | bytes 65536
  89.6 8.1 %copy.21 = bf16[1,2,8192]{2,1,0:T(2,128)(2,1)S(1)} copy(bf16[1,2,8192]{1,0,2:T(2,128)(2,1)} %bitcast.42) | data formatting | bytes 65536 | tf_op jit(solution)/shard_map/all_to_all | solution.py:11
  98.8 269.5 %all-gather.2.cloned.1.call-done = bf16[128,16,1024]{2,1,0:T(8,128)(2,1)} async-done(((bf16[1,16,1024]{2,1,0:T(8,128)(2,1)}), bf16[128,16,1024]{2,1,0:T(8,128)(2,1)}) %all-gather.2.cloned.1.call-update) | async-done | bytes 4194320 | tf_op jit(solution)/shard_map/all_gather | solution.py:17
  368.2 3.9 convolution_bitcast_fusion
  372.1 2.1 convolution_convert_fusion
  374.2 56.8 %while.14 = (s32[]{:T(128)}, f32[1024,128]{1,0:T(8,128)S(1)}, s32[2048,16]{1,0:T(8,128)S(1)}, s32[2048]{0:T(1024)}, bf16[2048,128]{1,0:T(8,128)(2,1)}, /*index=5*/s32[]{:T(128)}, s32[]{:T(128)}, s32[]{:T(128)}, s32[]{:T(128)}) while((s32[]{:T(128)}, f32[1024,128]{1,0:T(8,128)S(1)}, s32[2048,16]{1,0:T(8,128)S(1)}, s32[2048]{0:T(1024)}, ...), condition=%wide.region_2.0_spmd.clone, body=%wide.region_0.0_spmd.clone.sunk | while | flops 88084480 | bytes 2223273 | solution.py:45
  375.1 4.9 %convert_reduce_fusion.2 = bf16[256,1024]{1,0:T(8,128)(2,1)S(1)} fusion(s32[256,16]{1,0:T(8,128)S(1)} %constant_dynamic-slice_fusion.2, pred[256,16]{1,0:T(8,128)(4,1)S(1)} %iota_compare_fusion.3), kind=kLoop, calls=%fused_computation.2.clone.1 | loop fusion | flops 20709376 | bytes 544768 | tf_op jit(solution)/shard_map/while/body/eval_jaxpr/reduce_sum | solution.py:40
  382.2 4.9 %convert_reduce_fusion.2 = bf16[256,1024]{1,0:T(8,128)(2,1)S(1)} fusion(s32[256,16]{1,0:T(8,128)S(1)} %constant_dynamic-slice_fusion.2, pred[256,16]{1,0:T(8,128)(4,1)S(1)} %iota_compare_fusion.3), kind=kLoop, calls=%fused_computation.2.clone.1 | loop fusion | flops 20709376 | bytes 544768 | tf_op jit(solution)/shard_map/while/body/eval_jaxpr/reduce_sum | solution.py:40
  389.3 4.9 %convert_reduce_fusion.2 = bf16[256,1024]{1,0:T(8,128)(2,1)S(1)} fusion(s32[256,16]{1,0:T(8,128)S(1)} %constant_dynamic-slice_fusion.2, pred[256,16]{1,0:T(8,128)(4,1)S(1)} %iota_compare_fusion.3), kind=kLoop, calls=%fused_computation.2.clone.1 | loop fusion | flops 20709376 | bytes 544768 | tf_op jit(solution)/shard_map/while/body/eval_jaxpr/reduce_sum | solution.py:40
  394.2 1.3 convolution_add_fusion.2
  396.4 4.9 %convert_reduce_fusion.2 = bf16[256,1024]{1,0:T(8,128)(2,1)S(1)} fusion(s32[256,16]{1,0:T(8,128)S(1)} %constant_dynamic-slice_fusion.2, pred[256,16]{1,0:T(8,128)(4,1)S(1)} %iota_compare_fusion.3), kind=kLoop, calls=%fused_computation.2.clone.1 | loop fusion | flops 20709376 | bytes 544768 | tf_op jit(solution)/shard_map/while/body/eval_jaxpr/reduce_sum | solution.py:40
  401.3 1.3 convolution_add_fusion.2
  403.5 4.9 %convert_reduce_fusion.2 = bf16[256,1024]{1,0:T(8,128)(2,1)S(1)} fusion(s32[256,16]{1,0:T(8,128)S(1)} %constant_dynamic-slice_fusion.2, pred[256,16]{1,0:T(8,128)(4,1)S(1)} %iota_compare_fusion.3), kind=kLoop, calls=%fused_computation.2.clone.1 | loop fusion | flops 20709376 | bytes 544768 | tf_op jit(solution)/shard_map/while/body/eval_jaxpr/reduce_sum | solution.py:40
  408.4 1.3 convolution_add_fusion.2
  410.6 4.9 %convert_reduce_fusion.2 = bf16[256,1024]{1,0:T(8,128)(2,1)S(1)} fusion(s32[256,16]{1,0:T(8,128)S(1)} %constant_dynamic-slice_fusion.2, pred[256,16]{1,0:T(8,128)(4,1)S(1)} %iota_compare_fusion.3), kind=kLoop, calls=%fused_computation.2.clone.1 | loop fusion | flops 20709376 | bytes 544768 | tf_op jit(solution)/shard_map/while/body/eval_jaxpr/reduce_sum | solution.py:40
  417.7 4.9 %convert_reduce_fusion.2 = bf16[256,1024]{1,0:T(8,128)(2,1)S(1)} fusion(s32[256,16]{1,0:T(8,128)S(1)} %constant_dynamic-slice_fusion.2, pred[256,16]{1,0:T(8,128)(4,1)S(1)} %iota_compare_fusion.3), kind=kLoop, calls=%fused_computation.2.clone.1 | loop fusion | flops 20709376 | bytes 544768 | tf_op jit(solution)/shard_map/while/body/eval_jaxpr/reduce_sum | solution.py:40
  422.6 1.3 convolution_add_fusion.2
  424.8 4.9 %convert_reduce_fusion.2 = bf16[256,1024]{1,0:T(8,128)(2,1)S(1)} fusion(s32[256,16]{1,0:T(8,128)S(1)} %constant_dynamic-slice_fusion.2, pred[256,16]{1,0:T(8,128)(4,1)S(1)} %iota_compare_fusion.3), kind=kLoop, calls=%fused_computation.2.clone.1 | loop fusion | flops 20709376 | bytes 544768 | tf_op jit(solution)/shard_map/while/body/eval_jaxpr/reduce_sum | solution.py:40
  429.7 1.3 convolution_add_fusion.2
  431.0 2.2 fusion.9
  (45 shorter events, 12.6 us)
Async XLA Ops:
  7.2 361.1 %copy-start = (bf16[1,2048,128]{2,1,0:T(8,128)(2,1)S(1)}, bf16[1,2048,128]{2,1,0:T(8,128)(2,1)}, u32[]{:S(2)}) copy-start(bf16[1,2048,128]{2,1,0:T(8,128)(2,1)} %param.10) | copy-start | bytes 1572868
  7.2 361.0 %all-gather.2.cloned.1.call-start = ((), (), s32[]{:S(2)}) async-start(), calls=%async_computation.1 | async-start | bytes 4227072 | tf_op jit(solution)/shard_map/all_gather | solution.py:17
  83.4 15.1 %copy-start.3 = (s32[1,1,2048,16]{2,3,1,0:T(8,128)S(1)}, s32[1,1,2048,16]{2,3,1,0:T(8,128)}, u32[]{:S(2)}) copy-start(s32[1,1,2048,16]{2,3,1,0:T(8,128)} %param.12) | copy-start | bytes 393220
  97.7 274.4 %copy-start.4 = (bf16[1,128,1024]{2,1,0:T(8,128)(2,1)S(1)}, bf16[1,128,1024]{2,1,0:T(8,128)(2,1)}, u32[]{:S(2)}) copy-start(bf16[1,128,1024]{2,1,0:T(8,128)(2,1)} %param.11) | copy-start | bytes 786436
  368.2 3.9 copy-start.1
  374.2 56.8 %copy-start.2 = (f32[1,1024,128]{2,1,0:T(8,128)S(1)}, f32[1,1024,128]{2,1,0:T(8,128)}, u32[]{:S(2)}) copy-start(f32[1,1024,128]{2,1,0:T(8,128)} %param.15) | copy-start | bytes 1572868
Sparse Core Ops, SparseCore 0:
  98.5 269.6 all-gather.1
where the time goes:
time: 441 us; the launch traced here: 440 us
  waiting for transfers between devices  269 us (61%)
  other arithmetic  87.2 us (20%)
  local copies, waits for them, and re-layouts  33.7 us (8%)
  blocking collectives  18.9 us (4%)
  matrix products  16.3 us (4%)
  between operations  14.1 us (3%)
    all_gather x1, waiting for transfers between devices, per_device(): lax.all_gather(received, 'inner', axis=0, tiled=True).reshape(-1, width)  269 us
    unnamed x2, other arithmetic  45.2 us
    reduce_sum x8, other arithmetic, accumulate(): counts = jnp.sum(hits, axis=1, dtype=jnp.float32).astype(jnp.bfloat16)  38.9 us
    all_to_all x1, blocking collectives, per_device(): lax.all_to_all(grad_inter, 'tower', split_axis=2, concat_axis=1, tiled=True)  18.9 us
    unnamed x16, local copies, waits for them, and re-layouts  18.6 us
    dot_general x8, matrix products, accumulate(): lax.dot_general(counts, grad_block, (((0,), (0,)), ((), ())), preferred_e...  10.4 us
  transfers between devices with their start and end apart: 1, of which 1 were waited for; matrix products, arithmetic and copies ran while one was open for 0% of the time, Pallas kernels for 0%

commit v1 on v0

v1 whole, which is shorter than its diff:
```python
import functools

import jax
import jax.numpy as jnp
from jax import lax
from jax.experimental import pallas as pl
from jax.experimental.pallas import tpu as pltpu
from jax.sharding import Mesh, PartitionSpec as P

learn_rate = 0.1
epsilon = 1e-08

Z_PARTS = (4, 4, 2)
RING = ("a", "b")
BLOCK = ("c", "y")
INNER = ("a", "b", "c", "y")

BF16 = jnp.bfloat16
F32 = jnp.float32


def split_kernel(x_ref, o_ref):
    towers, _, width = o_ref.shape
    for t in range(towers):
        o_ref[t] = x_ref[:, t * width:(t + 1) * width]


def split_towers(x, towers):
    rows, width = x.shape
    return pl.pallas_call(
        split_kernel,
        out_shape=jax.ShapeDtypeStruct((towers, rows, width // towers), x.dtype),
    )(x)


def count_kernel(index_ref, length_ref, o_ref):
    bag, _ = index_ref.shape
    rows, lanes = o_ref.shape
    step = 16
    bag_at = lax.broadcasted_iota(jnp.int32, index_ref.shape, 0)
    live = jnp.where(bag_at < length_ref[...], index_ref[...], -1)
    entries = [
        jnp.broadcast_to(live[b:b + 1, :], (step, lanes)).astype(jnp.int16) for b in range(bag)
    ]
    first = lax.broadcasted_iota(jnp.int32, (step, lanes), 0)

    def body(k, _):
        low = pl.multiple_of(k * step, step)
        row = (first + low).astype(jnp.int16)
        parts = [jnp.where(e == row, jnp.ones((), BF16), jnp.zeros((), BF16)) for e in entries]
        while len(parts) > 1:
            parts = [parts[i] + parts[i + 1] for i in range(0, len(parts), 2)]
        o_ref[pl.ds(low, step), :] = parts[0]
        return 0

    lax.fori_loop(0, rows // step, body, 0, unroll=4)


def bag_counts(index_cols, bag_lengths, rows):
    bag, samples = index_cols.shape
    lanes = 128
    return pl.pallas_call(
        count_kernel,
        grid=(samples // lanes,),
        in_specs=[
            pl.BlockSpec((bag, lanes), lambda i: (0, i)),
            pl.BlockSpec((1, lanes), lambda i: (0, i)),
        ],
        out_specs=pl.BlockSpec((rows, lanes), lambda i: (0, i)),
        out_shape=jax.ShapeDtypeStruct((rows, samples), BF16),
        cost_estimate=pl.CostEstimate(
            flops=3 * bag * rows * samples, bytes_accessed=2 * rows * samples, transcendentals=0
        ),
    )(index_cols, bag_lengths)


def update_kernel(
    chunks, cot_ref, pooled_ref, weight_ref, counts_ref, slab_ref, sums_ref,
    wgrad_ref, table_ref, fresh_ref, pgrad_ref,
):
    k = pl.program_id(0)

    @pl.when(k == 0)
    def _():
        wgrad_ref[...] = jnp.zeros_like(wgrad_ref)

    @pl.when(k < chunks)
    def _():
        cot = cot_ref[0]
        rows = cot.shape[0]
        emb = weight_ref.shape[0]
        feats = pooled_ref[:, k].reshape(rows, emb)
        wgrad_ref[...] += lax.dot_general(
            feats, cot, (((0,), (0,)), ((), ())), preferred_element_type=F32
        )
        pgrad = lax.dot_general(
            cot, weight_ref[...], (((1,), (1,)), ((), ())), preferred_element_type=F32
        ).astype(BF16)
        pgrad_ref[:, k] = pgrad.reshape(pgrad_ref.shape[0], pgrad_ref.shape[2], emb)

    @pl.when(k >= chunks)
    def _():
        rows, lanes = pgrad_ref.shape[0] * pgrad_ref.shape[1] * pgrad_ref.shape[2], pgrad_ref.shape[3]
        row_grad = jnp.dot(
            counts_ref[...], pgrad_ref[...].reshape(rows, lanes), preferred_element_type=F32
        )
        fresh = sums_ref[...] + row_grad * row_grad
        fresh_ref[...] = fresh
        table_ref[...] = slab_ref[...] - learn_rate * row_grad / (jnp.sqrt(fresh) + epsilon)


def update(gathered, own, feats, weights, counts, slab, sums):
    chunks, rows, width = gathered.shape
    samples, emb = feats.shape
    groups = rows // own
    feats = feats.reshape(groups, chunks, own, emb)
    slab_rows = slab.shape[0]
    steps = 4
    tile = slab_rows // steps
    first = lambda k: jnp.minimum(k, chunks - 1)
    second = lambda k: jnp.maximum(k - chunks, 0)
    return pl.pallas_call(
        functools.partial(update_kernel, chunks),
        grid=(chunks + steps,),
        in_specs=[
            pl.BlockSpec((1, rows, width), lambda k: (first(k), 0, 0)),
            pl.BlockSpec((groups, chunks, own, emb), lambda k: (0, 0, 0, 0)),
            pl.BlockSpec((emb, width), lambda k: (0, 0)),
            pl.BlockSpec((tile, samples), lambda k: (second(k), 0)),
            pl.BlockSpec((tile, emb), lambda k: (second(k), 0)),
            pl.BlockSpec((tile, emb), lambda k: (second(k), 0)),
        ],
        out_specs=[
            pl.BlockSpec((emb, width), lambda k: (0, 0)),
            pl.BlockSpec((tile, emb), lambda k: (second(k), 0)),
            pl.BlockSpec((tile, emb), lambda k: (second(k), 0)),
        ],
        out_shape=[
            jax.ShapeDtypeStruct((emb, width), F32),
            jax.ShapeDtypeStruct((slab_rows, emb), F32),
            jax.ShapeDtypeStruct((slab_rows, emb), F32),
        ],
        scratch_shapes=[pltpu.VMEM((groups, chunks, own, emb), BF16)],
        compiler_params=pltpu.CompilerParams(vmem_limit_bytes=32 * 1024 * 1024),
        cost_estimate=pl.CostEstimate(
            flops=4 * samples * emb * width + 2 * samples * emb * slab_rows,
            bytes_accessed=2 * samples * (width + slab_rows) + 16 * slab_rows * emb,
            transcendentals=slab_rows * emb,
        ),
    )(gathered, feats, weights, counts, slab, sums)


def per_device(grad_inter, pooled, tower_weight, indices, lengths, table_slab, accumulator):
    towers = lax.axis_size("tower")
    members = lax.axis_size(BLOCK)
    counts = bag_counts(indices[0, 0].T, lengths[0], table_slab.shape[1])
    parted = split_towers(grad_inter[0], towers)
    own = lax.all_to_all(parted, "tower", split_axis=0, concat_axis=0)
    own = own.reshape(-1, own.shape[2])
    ring = lax.all_gather(own, RING, axis=0, tiled=True)
    gathered = lax.all_to_all(
        jnp.broadcast_to(ring[None], (members,) + ring.shape), BLOCK, split_axis=0, concat_axis=0
    )
    wgrad, updated, fresh = update(
        gathered, own.shape[0], pooled[0], tower_weight[0], counts, table_slab[0], accumulator[0]
    )
    return (wgrad[None], updated[None], fresh[None])


def solution(mesh):
    towers, inner = mesh.devices.shape
    shape = (towers,) + Z_PARTS + (inner // (Z_PARTS[0] * Z_PARTS[1] * Z_PARTS[2]),)
    fine = Mesh(mesh.devices.reshape(shape), ("tower",) + INNER)
    return jax.shard_map(
        per_device,
        mesh=fine,
        in_specs=(
            P(INNER, "tower", None),
            P("tower", None, INNER),
            P("tower", INNER, None),
            P("tower", INNER, None, None),
            P("tower", INNER, None),
            P("tower", INNER, None),
            P("tower", INNER, None),
        ),
        out_specs=(P("tower", INNER, None), P("tower", INNER, None), P("tower", INNER, None)),
        check_vma=False,
    )
```

time: 441 us -> 124 us (0.28)
  the two profiles are of different devices: /device:TPU:6 before, /device:TPU:32 now
where the time goes in v1:
time: 124 us; the launch traced here: 123 us
  blocking collectives  59.5 us (48%)
  waiting for transfers between devices  29 us (23%)
  Pallas kernels  23.1 us (19%)
  starting transfers between devices  5.93 us (5%)
  local copies, waits for them, and re-layouts  4.74 us (4%)
    all_gather x1, blocking collectives, per_device(): ring = lax.all_gather(own, RING, axis=0, tiled=True)  49.7 us
    all_to_all x1, waiting for transfers between devices, per_device(): lax.all_to_all(jnp.broadcast_to(ring[None], (members,) + ring.shape), BLO...  29 us
    pallas_call x1, Pallas kernels, bag_counts(): pl.pallas_call(count_kernel, grid=(samples // lanes,), in_specs=[pl.Block...  12.2 us
    all_to_all x1, blocking collectives, per_device(): own = lax.all_to_all(parted, 'tower', split_axis=0, concat_axis=0)  9.74 us
    pallas_call x1, Pallas kernels, update(): pl.pallas_call(functools.partial(update_kernel, chunks), grid=(chunks + s...  9.53 us
    all_to_all x1, starting transfers between devices, per_device(): lax.all_to_all(jnp.broadcast_to(ring[None], (members,) + ring.shape), BLO...  5.93 us
    broadcast_in_dim x1, local copies, waits for them, and re-layouts, per_device(): jnp.broadcast_to(ring[None], (members,) + ring.shape)  2.52 us
  transfers between devices with their start and end apart: 1, of which 1 were waited for; matrix products, arithmetic and copies ran while one was open for 0% of the time, Pallas kernels for 10%

profile of v1, /device:TPU:32, one launch (start us, length us, event | category | flops | bytes accessed | tf_op | source)
XLA Modules:
  0.0 122.9 jit_solution(4354173058958433074)
XLA Ops:
  0.6 1.4 %shard_map.94 = bf16[8,2,1024]{2,1,0:T(2,128)(2,1)} custom-call(bf16[2,8192]{1,0:T(2,128)(2,1)} %bitcast.17), custom_call_target="tpu_custom_call" | custom-call | tf_op jit(solution)/shard_map/pallas_call | solution.py:30
  2.0 9.7 %all_to_all.10 = bf16[8,2,1024]{2,1,0:T(2,128)(2,1)S(1)} all-to-all(bf16[8,2,1024]{2,1,0:T(2,128)(2,1)} %shard_map.94), channel_id=1, replica_groups=mesh['tower'=8,'a'=4,'b'=4,'c'=2,'y'=4] {'tower'}, dimensions={0} | all-to-all | bytes 65536 | tf_op jit(solution)/shard_map/all_to_all | solution.py:158
  11.8 49.7 %all_gather.3 = bf16[256,1024]{1,0:T(8,128)(2,1)S(1)} all-gather(bf16[16,1024]{1,0:T(8,128)(2,1)S(1)} %reshape.10), channel_id=1, replica_groups=mesh['tower'=8,'a'=4,'b'=4,'c'=2,'y'=4] {'a','b'}, dimensions={0}, use_global_device_ids=true | all-gather | bytes 557056 | tf_op jit(solution)/shard_map/all_gather | solution.py:160
  61.5 2.5 %broadcast_in_dim.15 = bf16[8,256,1024]{2,1,0:T(8,128)(2,1)} broadcast(bf16[256,1024]{1,0:T(8,128)(2,1)S(1)} %all_gather.3), dimensions={1,2} | broadcast | bytes 4718592 | tf_op jit(solution)/shard_map/broadcast_in_dim | solution.py:162
  64.0 5.9 %all-to-all-start.1 = ((bf16[8,256,1024]{2,1,0:T(8,128)(2,1)}), bf16[8,256,1024]{2,1,0:T(8,128)(2,1)}, u32[]{:S(2)}, u32[]{:S(2)}) async-start(bf16[8,256,1024]{2,1,0:T(8,128)(2,1)} %broadcast_in_dim.15), calls=%async_computation.1 | async-start | bytes 8388608 | tf_op jit(solution)/shard_map/all_to_all | solution.py:161
  70.0 0.0 copy-start.1
  70.0 0.0 copy-start.2
  70.0 0.0 copy-start.3
  70.0 0.0 copy-start.4
  70.0 12.2 %shard_map.95.counts_ref = bf16[1024,2048]{1,0:T(8,128)(2,1)} custom-call(s32[16,2048]{1,0:T(8,128)} %bitcast.16, s32[1,2048]{1,0:T(1,128)} %bitcast.18), custom_call_target="tpu_custom_call" | custom-call | flops 100663296 | bytes 4194304 | tf_op jit(solution)/shard_map/pallas_call | solution.py:62
  82.1 29.0 %all-to-all-done.1.cot_ref = bf16[8,256,1024]{2,1,0:T(8,128)(2,1)} async-done(((bf16[8,256,1024]{2,1,0:T(8,128)(2,1)}), bf16[8,256,1024]{2,1,0:T(8,128)(2,1)}, u32[]{:S(2)}, u32[]{:S(2)}) %all-to-all-start.1) | async-done | bytes 4194336 | tf_op jit(solution)/shard_map/all_to_all | solution.py:161
  111.2 0.0 copy-done.1
  111.2 0.0 copy-done.2
  111.2 0.0 copy-done.3
  111.2 0.0 copy-done.4
  111.2 0.0 copy-start
  111.2 2.2 %copy-done = bf16[1024,2048]{1,0:T(8,128)(2,1)S(1)} copy-done((bf16[1024,2048]{1,0:T(8,128)(2,1)S(1)}, bf16[1024,2048]{1,0:T(8,128)(2,1)}, u32[]{:S(2)}) %copy-start) | copy-done | bytes 4194328
  113.4 9.5 %shard_map.96 = (f32[128,1024]{1,0:T(8,128)}, f32[1024,128]{1,0:T(8,128)}, f32[1024,128]{1,0:T(8,128)}) custom-call(bf16[8,256,1024]{2,1,0:T(8,128)(2,1)} %all-to-all-done.1.cot_ref, bf16[16,8,16,128]{3,2,1,0:T(8,128)(2,1)S(1)} %bitcast.12, bf16[128,1024]{1,0:T(8,128)(2,1)S(1)} %bitcast.15, bf16[1024,2048]{1,0:T(8,128)(2,1)S(1)} %copy-done, ...), custom_call_target="tpu_custom_call" | custom-call | flops 1610612736 | bytes 10485760 | tf_op jit(solution)/shard_map/pallas_call | solution.py:122
  (1 shorter events, 0.0 us)
Async XLA Ops:
  64.0 47.1 %all-to-all-start.1 = ((bf16[8,256,1024]{2,1,0:T(8,128)(2,1)}), bf16[8,256,1024]{2,1,0:T(8,128)(2,1)}, u32[]{:S(2)}, u32[]{:S(2)}) async-start(bf16[8,256,1024]{2,1,0:T(8,128)(2,1)} %broadcast_in_dim.15), calls=%async_computation.1 | async-start | bytes 8388608 | tf_op jit(solution)/shard_map/all_to_all | solution.py:161
  70.0 41.2 %copy-start.1 = (bf16[1,2048,128]{2,1,0:T(8,128)(2,1)S(1)}, bf16[1,2048,128]{2,1,0:T(8,128)(2,1)}, u32[]{:S(2)}) copy-start(bf16[1,2048,128]{2,1,0:T(8,128)(2,1)} %param.8) | copy-start | bytes 1572868
  70.0 41.2 %copy-start.2 = (f32[1,1024,128]{2,1,0:T(8,128)S(1)}, f32[1,1024,128]{2,1,0:T(8,128)}, u32[]{:S(2)}) copy-start(f32[1,1024,128]{2,1,0:T(8,128)} %param.12) | copy-start | bytes 1572868
  70.0 41.2 %copy-start.3 = (f32[1,1024,128]{2,1,0:T(8,128)S(1)}, f32[1,1024,128]{2,1,0:T(8,128)}, u32[]{:S(2)}) copy-start(f32[1,1024,128]{2,1,0:T(8,128)} %param.13) | copy-start | bytes 1572868
  70.0 41.2 %copy-start.4 = (bf16[1,128,1024]{2,1,0:T(8,128)(2,1)S(1)}, bf16[1,128,1024]{2,1,0:T(8,128)(2,1)}, u32[]{:S(2)}) copy-start(bf16[1,128,1024]{2,1,0:T(8,128)(2,1)} %param.9) | copy-start | bytes 786436
  111.2 2.2 %copy-start = (bf16[1024,2048]{1,0:T(8,128)(2,1)S(1)}, bf16[1024,2048]{1,0:T(8,128)(2,1)}, u32[]{:S(2)}) copy-start(bf16[1024,2048]{1,0:T(8,128)(2,1)} %shard_map.95.counts_ref) | copy-start | bytes 12582916

commit v2 on v1

v2 whole, which is shorter than its diff:
```python
import functools

import jax
import jax.numpy as jnp
from jax import lax
from jax.experimental import pallas as pl
from jax.experimental.pallas import tpu as pltpu
from jax.sharding import Mesh, PartitionSpec as P

learn_rate = 0.1
epsilon = 1e-08

HALVES = 2
RING, HALF, SIDE = "ring", "half", "side"
INNER = (RING, HALF, SIDE)
PAIRED = ("tower", RING, HALF)

BF16 = jnp.bfloat16
F32 = jnp.float32
LIMIT = pltpu.CompilerParams(vmem_limit_bytes=20 * 1024 * 1024)


def partners(towers, length):
    pairs = []
    for t in range(towers):
        for z in range(length):
            up = (z + t) % 2 == 0
            pairs.append((t * length + z, t * length + (z + (1 if up else -1)) % length))
    return pairs


def across(w):
    rows, cols = w.shape
    return jnp.concatenate([w[:, i:i + rows] for i in range(0, cols, rows)], axis=0)


def along(w, rows):
    return jnp.concatenate([w[i:i + rows] for i in range(0, w.shape[0], rows)], axis=1)


def prepare_kernel(half_ref, x_ref, pooled_ref, weight_ref, o_ref, send_ref):
    towers, _, width = o_ref.shape
    for t in range(towers):
        o_ref[t] = x_ref[:, t * width:(t + 1) * width]
    send_ref[0] = pooled_ref[:, 0]
    send_ref[1] = across(weight_ref[...]).reshape(send_ref.shape[1:])


def prepare(half, x, towers, feats, weights):
    rows, width = x.shape
    ring, halves, sides, own, emb = feats.shape
    return pl.pallas_call(
        prepare_kernel,
        grid_spec=pltpu.PrefetchScalarGridSpec(
            num_scalar_prefetch=1,
            grid=(1,),
            in_specs=[
                pl.BlockSpec(x.shape, lambda k, h: (0, 0)),
                pl.BlockSpec((ring, 1, sides, own, emb), lambda k, h: (0, 1 - h[0], 0, 0, 0)),
                pl.BlockSpec(weights.shape, lambda k, h: (0, 0)),
            ],
            out_specs=[
                pl.BlockSpec((towers, rows, width // towers), lambda k, h: (0, 0, 0)),
                pl.BlockSpec((2, ring, sides, own, emb), lambda k, h: (0, 0, 0, 0, 0)),
            ],
        ),
        out_shape=[
            jax.ShapeDtypeStruct((towers, rows, width // towers), BF16),
            jax.ShapeDtypeStruct((2, ring, sides, own, emb), BF16),
        ],
    )(half, x, feats, weights)


def count_kernel(half_ref, index_ref, length_ref, o_ref, done_ref):
    done_ref[...] = jnp.zeros_like(done_ref)
    bag, width = index_ref.shape
    _, rows, lanes = o_ref.shape
    step = 16
    run = lanes // 2
    bag_at = lax.broadcasted_iota(jnp.int32, index_ref.shape, 0)
    live = jnp.where(bag_at < length_ref[...], index_ref[...], -1)
    left, right = live[:, :lanes], live[:, lanes:]
    low_lane = lax.broadcasted_iota(jnp.int32, left.shape, 1) < run
    halves = [
        jnp.where(low_lane, left, pltpu.roll(right, run, 1)),
        jnp.where(low_lane, pltpu.roll(left, run, 1), right),
    ]
    upper = half_ref[0] == 1
    first = lax.broadcasted_iota(jnp.int32, (step, lanes), 0)
    for side in range(2):
        chosen = jnp.where(upper, halves[1 - side], halves[side])
        entries = [
            jnp.broadcast_to(chosen[b:b + 1, :], (step, lanes)).astype(jnp.int16)
            for b in range(bag)
        ]

        def body(k, _, entries=entries, side=side):
            low = pl.multiple_of(k * step, step)
            row = (first + low).astype(jnp.int16)
            parts = [jnp.where(e == row, jnp.ones((), BF16), jnp.zeros((), BF16)) for e in entries]
            while len(parts) > 1:
                parts = [parts[i] + parts[i + 1] for i in range(0, len(parts), 2)]
            o_ref[side, pl.ds(low, step), :] = parts[0]
            return 0

        lax.fori_loop(0, rows // step, body, 0, unroll=4)


def bag_counts(half, index_cols, bag_lengths, rows):
    bag, samples = index_cols.shape
    lanes = 128
    return pl.pallas_call(
        count_kernel,
        grid_spec=pltpu.PrefetchScalarGridSpec(
            num_scalar_prefetch=1,
            grid=(samples // (HALVES * lanes),),
            in_specs=[
                pl.BlockSpec((bag, HALVES * lanes), lambda i, h: (0, i)),
                pl.BlockSpec((1, HALVES * lanes), lambda i, h: (0, i)),
            ],
            out_specs=[
                pl.BlockSpec((HALVES, rows, lanes), lambda i, h: (0, 0, i)),
                pl.BlockSpec((8, 128), lambda i, h: (0, 0)),
            ],
        ),
        out_shape=[
            jax.ShapeDtypeStruct((HALVES, rows, samples // HALVES), BF16),
            jax.ShapeDtypeStruct((8, 128), F32),
        ],
        compiler_params=LIMIT,
        cost_estimate=pl.CostEstimate(
            flops=3 * bag * rows * samples, bytes_accessed=2 * rows * samples, transcendentals=0
        ),
    )(half, index_cols, bag_lengths)


def products(cot, feats, weights):
    wgrad = lax.dot_general(feats, cot, (((0,), (0,)), ((), ())), preferred_element_type=F32)
    pgrad = lax.dot_general(cot, weights, (((1,), (1,)), ((), ())), preferred_element_type=F32)
    return wgrad, pgrad.astype(BF16)


def partner_kernel(cot_ref, feats_ref, weight_ref, counted_ref, o_ref, total_ref):
    del counted_ref
    k = pl.program_id(0)
    cot = cot_ref[0]
    emb, width = total_ref.shape
    weights = along(weight_ref[0].reshape(width, emb), emb)
    wgrad, pgrad = products(cot, feats_ref[...].reshape(cot.shape[0], emb), weights)
    ring, own = o_ref.shape[1], o_ref.shape[3]
    o_ref[0, :, k] = pgrad.reshape(ring, own, emb)

    @pl.when(k == 0)
    def _():
        total_ref[...] = wgrad

    @pl.when(k > 0)
    def _():
        total_ref[...] += wgrad

    @pl.when(k == pl.num_programs(0) - 1)
    def _():
        o_ref[1] = across(total_ref[...].astype(BF16)).reshape(o_ref.shape[1:])


def partner_part(gathered, received, counted):
    sides, rows, width = gathered.shape
    _, ring, _, own, emb = received.shape
    return pl.pallas_call(
        partner_kernel,
        grid=(sides,),
        in_specs=[
            pl.BlockSpec((1, rows, width), lambda k: (k, 0, 0)),
            pl.BlockSpec((1, ring, 1, own, emb), lambda k: (0, 0, k, 0, 0)),
            pl.BlockSpec((1, ring, sides, own, emb), lambda k: (1, 0, 0, 0, 0)),
            pl.BlockSpec(memory_space=pl.ANY),
        ],
        out_specs=pl.BlockSpec(received.shape, lambda k: (0, 0, 0, 0, 0)),
        out_shape=jax.ShapeDtypeStruct(received.shape, BF16),
        scratch_shapes=[pltpu.VMEM((emb, width), F32)],
        compiler_params=LIMIT,
        cost_estimate=pl.CostEstimate(
            flops=4 * sides * rows * emb * width,
            bytes_accessed=2 * sides * rows * width + 4 * received.size,
            transcendentals=0,
        ),
    )(gathered, received, received, counted)


def own_kernel(
    half_ref, cot_ref, feats_ref, weight_ref, counts_ref, wgrad_ref, row_ref, pgrad_ref
):
    k = pl.program_id(0)
    cot = cot_ref[0]
    emb = weight_ref.shape[0]
    ring, sides, own, _ = pgrad_ref.shape
    wgrad, pgrad = products(cot, feats_ref[...].reshape(cot.shape[0], emb), weight_ref[...])
    pgrad_ref[:, k] = pgrad.reshape(ring, own, emb)

    @pl.when(k == 0)
    def _():
        wgrad_ref[...] = wgrad

    @pl.when(k > 0)
    def _():
        wgrad_ref[...] += wgrad

    @pl.when(k == pl.num_programs(0) - 1)
    def _():
        row_ref[...] = jnp.dot(
            counts_ref[0],
            pgrad_ref[...].reshape(ring * sides * own, emb),
            preferred_element_type=F32,
        )


def own_part(half, gathered, feats, weights, counts):
    sides, rows, width = gathered.shape
    ring, _, _, own, emb = feats.shape
    _, table_rows, samples = counts.shape
    return pl.pallas_call(
        own_kernel,
        grid_spec=pltpu.PrefetchScalarGridSpec(
            num_scalar_prefetch=1,
            grid=(sides,),
            in_specs=[
                pl.BlockSpec((1, rows, width), lambda k, h: (k, 0, 0)),
                pl.BlockSpec((ring, 1, 1, own, emb), lambda k, h: (0, h[0], k, 0, 0)),
                pl.BlockSpec((emb, width), lambda k, h: (0, 0)),
                pl.BlockSpec((1, table_rows, samples), lambda k, h: (0, 0, 0)),
            ],
            out_specs=[
                pl.BlockSpec((emb, width), lambda k, h: (0, 0)),
                pl.BlockSpec((table_rows, emb), lambda k, h: (0, 0)),
            ],
            scratch_shapes=[pltpu.VMEM((ring, sides, own, emb), BF16)],
        ),
        out_shape=[
            jax.ShapeDtypeStruct((emb, width), F32),
            jax.ShapeDtypeStruct((table_rows, emb), F32),
        ],
        compiler_params=LIMIT,
        cost_estimate=pl.CostEstimate(
            flops=4 * sides * rows * emb * width + 2 * samples * emb * table_rows,
            bytes_accessed=2 * sides * rows * width + 8 * emb * width,
            transcendentals=0,
        ),
    )(half, gathered, feats, weights, counts)


def update_kernel(
    other_ref, share_ref, row_ref, counts_ref, slab_ref, sums_ref,
    wgrad_ref, table_ref, fresh_ref,
):
    _, ring, sides, own, emb = other_ref.shape

    @pl.when(pl.program_id(0) == 0)
    def _():
        width = share_ref.shape[1]
        wgrad_ref[...] = share_ref[...] + along(other_ref[1].reshape(width, emb), emb).astype(F32)

    row_grad = row_ref[...] + jnp.dot(
        counts_ref[0],
        other_ref[0].reshape(ring * sides * own, emb),
        preferred_element_type=F32,
    )
    fresh = sums_ref[...] + row_grad * row_grad
    fresh_ref[...] = fresh
    table_ref[...] = slab_ref[...] - learn_rate * row_grad / (jnp.sqrt(fresh) + epsilon)


def update(other, share, row_share, counts, slab, sums):
    _, rows, samples = counts.shape
    emb, width = share.shape
    steps = 4
    tile = rows // steps
    return pl.pallas_call(
        update_kernel,
        grid=(steps,),
        in_specs=[
            pl.BlockSpec(other.shape, lambda k: (0, 0, 0, 0, 0)),
            pl.BlockSpec((emb, width), lambda k: (0, 0)),
            pl.BlockSpec((tile, emb), lambda k: (k, 0)),
            pl.BlockSpec((1, tile, samples), lambda k: (1, k, 0)),
            pl.BlockSpec((tile, emb), lambda k: (k, 0)),
            pl.BlockSpec((tile, emb), lambda k: (k, 0)),
        ],
        out_specs=[
            pl.BlockSpec((emb, width), lambda k: (0, 0)),
            pl.BlockSpec((tile, emb), lambda k: (k, 0)),
            pl.BlockSpec((tile, emb), lambda k: (k, 0)),
        ],
        out_shape=[
            jax.ShapeDtypeStruct((emb, width), F32),
            jax.ShapeDtypeStruct((rows, emb), F32),
            jax.ShapeDtypeStruct((rows, emb), F32),
        ],
        compiler_params=LIMIT,
        cost_estimate=pl.CostEstimate(
            flops=2 * samples * emb * rows,
            bytes_accessed=2 * samples * rows + 16 * rows * emb + 12 * emb * width,
            transcendentals=rows * emb,
        ),
    )(other, share, row_share, counts, slab, sums)


def per_device(grad_inter, pooled, tower_weight, indices, lengths, table_slab, accumulator):
    towers, ring_size, sides = (lax.axis_size(a) for a in ("tower", RING, SIDE))
    pairs = partners(towers, ring_size * HALVES)
    half = lax.axis_index(HALF).astype(jnp.int32).reshape(1)
    weights = tower_weight[0]
    feats = pooled[0].reshape(ring_size, HALVES, sides, -1, pooled.shape[2])

    parted, to_partner = prepare(half, grad_inter[0], towers, feats, weights)
    from_partner = lax.ppermute(to_partner, PAIRED, pairs)
    own = lax.all_to_all(parted, "tower", split_axis=0, concat_axis=0)
    own = own.reshape(-1, own.shape[2])
    ring = lax.all_gather(own, RING, axis=0, tiled=True)
    gathered = lax.all_to_all(
        jnp.broadcast_to(ring[None], (sides,) + ring.shape), SIDE, split_axis=0, concat_axis=0
    )
    counts, counted = bag_counts(half, indices[0, 0].T, lengths[0], table_slab.shape[1])

    other = lax.ppermute(partner_part(gathered, from_partner, counted), PAIRED, pairs)
    share, row_share = own_part(half, gathered, feats, weights, counts)
    wgrad, updated, fresh = update(
        other, share, row_share, counts, table_slab[0], accumulator[0]
    )
    return (wgrad[None], updated[None], fresh[None])


def solution(mesh):
    towers, inner = mesh.devices.shape
    ring_size, sides = 16, 4
    fine = Mesh(
        mesh.devices.reshape(towers, ring_size, HALVES, sides), ("tower",) + INNER
    )
    return jax.shard_map(
        per_device,
        mesh=fine,
        in_specs=(
            P(INNER, "tower", None),
            P("tower", None, INNER),
            P("tower", INNER, None),
            P("tower", INNER, None, None),
            P("tower", INNER, None),
            P("tower", INNER, None),
            P("tower", INNER, None),
        ),
        out_specs=(P("tower", INNER, None), P("tower", INNER, None), P("tower", INNER, None)),
        check_vma=False,
    )
```

time: 124 us -> 104 us (0.84)
  waiting for transfers between devices: 29 us -> 7.3 us
  starting transfers between devices: 5.93 us -> 10.4 us
  Pallas kernels: 23.1 us -> 19.4 us
    all_to_all x1, waiting for transfers between devices: 29 us -> 3.7 us  [per_device(): lax.all_to_all(jnp.broadcast_to(ring[None], (sides,) + ring.shape), SIDE,...]
    ppermute x0 -> x2, starting transfers between devices: none -> 5.81 us  [the longest x1 3.15 us: per_device(): from_partner = lax.ppermute(to_partner, PAIRED, pairs)]
    pallas_call x3 -> x5, Pallas kernels: 23.1 us -> 19.4 us  [the longest x1 10.6 us: bag_counts(): pl.pallas_call(count_kernel, grid_spec=pltpu.PrefetchScalarGridSpec(num_s...]
    ppermute x0 -> x2, waiting for transfers between devices: none -> 3.6 us  [the longest x1 3.6 us: per_device(): lax.ppermute(partner_part(gathered, from_partner, counted), PAIRED, pairs)]
    unnamed x10 -> x18, local copies, waits for them, and re-layouts: 2.2 us -> 4.17 us
    all_to_all x1, starting transfers between devices: 5.93 us -> 4.59 us  [per_device(): lax.all_to_all(jnp.broadcast_to(ring[None], (sides,) + ring.shape), SIDE,...]
  transfers between devices with their start and end apart: 1 -> 3, of which waited for: 1 -> 2; matrix products, arithmetic and copies ran while one was open for 0% -> 0% of each run, Pallas kernels for 10% -> 13%
where the time goes in v2:
time: 104 us; the launch traced here: 103 us
  blocking collectives  59.5 us (57%)
  Pallas kernels  19.4 us (19%)
  starting transfers between devices  10.4 us (10%)
  waiting for transfers between devices  7.3 us (7%)
  local copies, waits for them, and re-layouts  5.83 us (6%)
    all_gather x1, blocking collectives, per_device(): ring = lax.all_gather(own, RING, axis=0, tiled=True)  49.7 us
    pallas_call x1, Pallas kernels, bag_counts(): pl.pallas_call(count_kernel, grid_spec=pltpu.PrefetchScalarGridSpec(num_s...  10.6 us
    all_to_all x1, blocking collectives, per_device(): own = lax.all_to_all(parted, 'tower', split_axis=0, concat_axis=0)  9.74 us
    all_to_all x1, starting transfers between devices, per_device(): lax.all_to_all(jnp.broadcast_to(ring[None], (sides,) + ring.shape), SIDE,...  4.59 us
    unnamed x18, local copies, waits for them, and re-layouts  4.17 us
    all_to_all x1, waiting for transfers between devices, per_device(): lax.all_to_all(jnp.broadcast_to(ring[None], (sides,) + ring.shape), SIDE,...  3.7 us
    ppermute x1, waiting for transfers between devices, per_device(): lax.ppermute(partner_part(gathered, from_partner, counted), PAIRED, pairs)  3.6 us
    ppermute x1, starting transfers between devices, per_device(): from_partner = lax.ppermute(to_partner, PAIRED, pairs)  3.15 us
  transfers between devices with their start and end apart: 3, of which 2 were waited for; matrix products, arithmetic and copies ran while one was open for 0% of the time, Pallas kernels for 13%

profile of v2, /device:TPU:32, one launch (start us, length us, event | category | flops | bytes accessed | tf_op | source)
XLA Modules:
  0.0 103.2 jit_solution(6953235543559065381)
XLA Ops:
  0.6 1.9 %shard_map.94 = (bf16[8,2,1024]{2,1,0:T(2,128)(2,1)}, bf16[2,16,4,16,128]{4,3,2,1,0:T(8,128)(2,1)}) custom-call(s32[1]{0:T(128)} %bitcast.half_ref, bf16[2,8192]{1,0:T(2,128)(2,1)} %bitcast.21, bf16[16,2,4,16,128]{4,3,2,1,0:T(8,128)(2,1)} %bitcast.13, bf16[128,1024]{1,0:T(8,128)(2,1)} %bitcast.15), custom_call_target="tpu_custom_call" | custom-call | tf_op jit(solution)/shard_map/pallas_call | solution.py:52
  2.5 9.7 %all_to_all.10 = bf16[8,2,1024]{2,1,0:T(2,128)(2,1)S(1)} all-to-all(bf16[8,2,1024]{2,1,0:T(2,128)(2,1)} %get-tuple-element.12), channel_id=1, replica_groups=mesh['tower'=8,'ring'=16,'half'=2,'side'=4] {'tower'}, dimensions={0} | all-to-all | bytes 65536 | tf_op jit(solution)/shard_map/all_to_all | solution.py:316
  12.3 49.7 %all_gather.3 = bf16[256,1024]{1,0:T(8,128)(2,1)S(1)} all-gather(bf16[16,1024]{1,0:T(8,128)(2,1)S(1)} %reshape.14), channel_id=1, replica_groups=mesh['tower'=8,'ring'=16,'half'=2,'side'=4] {'ring'}, dimensions={0}, use_global_device_ids=true | all-gather | bytes 557056 | tf_op jit(solution)/shard_map/all_gather | solution.py:318
  62.0 1.6 %broadcast_in_dim.15 = bf16[4,256,1024]{2,1,0:T(8,128)(2,1)} broadcast(bf16[256,1024]{1,0:T(8,128)(2,1)S(1)} %all_gather.3), dimensions={1,2} | broadcast | bytes 2621440 | tf_op jit(solution)/shard_map/broadcast_in_dim | solution.py:320
  63.7 4.6 %all-to-all-start.1 = ((bf16[4,256,1024]{2,1,0:T(8,128)(2,1)}), bf16[4,256,1024]{2,1,0:T(8,128)(2,1)S(1)}, u32[]{:S(2)}, u32[]{:S(2)}) async-start(bf16[4,256,1024]{2,1,0:T(8,128)(2,1)} %broadcast_in_dim.15), calls=%async_computation.1 | async-start | bytes 4194304 | tf_op jit(solution)/shard_map/all_to_all | solution.py:319
  68.3 3.1 %collective-permute-start = (bf16[2,16,4,16,128]{4,3,2,1,0:T(8,128)(2,1)}, bf16[2,16,4,16,128]{4,3,2,1,0:T(8,128)(2,1)S(1)}, u32[]{:S(2)}, u32[]{:S(2)}) collective-permute-start(bf16[2,16,4,16,128]{4,3,2,1,0:T(8,128)(2,1)} %get-tuple-element.13), channel_id=1, source_target_pairs={{0,4},{4,0},{8,12},{12,8},{16,20},{20,16},{24,28},{28,24},{32,36},... | collective-permute-start | bytes 1572872 | tf_op jit(solution)/shard_map/ppermute | solution.py:315
  71.4 0.0 copy-done.7
  71.5 0.0 copy-done.8
  71.5 10.6 %shard_map.95 = (bf16[2,1024,1024]{2,1,0:T(8,128)(2,1)S(1)}, f32[8,128]{1,0:T(8,128)S(1)}) custom-call(s32[1]{0:T(128)} %bitcast.half_ref, s32[16,2048]{1,0:T(8,128)S(1)} %bitcast.19, s32[1,2048]{1,0:T(1,128)S(1)} %bitcast.20), custom_call_target="tpu_custom_call" | custom-call | flops 100663296 | bytes 4194304 | tf_op jit(solution)/shard_map/pallas_call | solution.py:112
  82.1 0.0 copy-start
  82.1 2.0 %copy-done = bf16[2,1024,1024]{2,1,0:T(8,128)(2,1)} copy-done((bf16[2,1024,1024]{2,1,0:T(8,128)(2,1)}, bf16[2,1024,1024]{2,1,0:T(8,128)(2,1)S(1)}, u32[]{:S(2)}) %copy-start) | copy-done | bytes 4194328
  84.1 0.0 collective-permute-done.feats_ref.weight_ref
  84.1 3.7 %all-to-all-done.1.cot_ref = bf16[4,256,1024]{2,1,0:T(8,128)(2,1)S(1)} async-done(((bf16[4,256,1024]{2,1,0:T(8,128)(2,1)}), bf16[4,256,1024]{2,1,0:T(8,128)(2,1)S(1)}, u32[]{:S(2)}, u32[]{:S(2)}) %all-to-all-start.1) | async-done | bytes 2097184 | tf_op jit(solution)/shard_map/all_to_all | solution.py:319
  87.8 1.9 %shard_map.96 = bf16[2,16,4,16,128]{4,3,2,1,0:T(8,128)(2,1)S(1)} custom-call(bf16[4,256,1024]{2,1,0:T(8,128)(2,1)S(1)} %all-to-all-done.1.cot_ref, bf16[2,16,4,16,128]{4,3,2,1,0:T(8,128)(2,1)S(1)} %collective-permute-done.feats_ref.weight_ref, bf16[2,16,4,16,128]{4,3,2,1,0:T(8,128)(2,1)S(1)} %collective-permute-done.feats_ref.weight_ref, ...), custom_call_target="tpu_custom_call" | custom-call | flops 536870912 | bytes 3145728 | tf_op jit(solution)/shard_map/pallas_call | solution.py:169
  89.7 2.7 %collective-permute-start.1 = (bf16[2,16,4,16,128]{4,3,2,1,0:T(8,128)(2,1)S(1)}, bf16[2,16,4,16,128]{4,3,2,1,0:T(8,128)(2,1)S(1)}, u32[]{:S(2)}, u32[]{:S(2)}) collective-permute-start(bf16[2,16,4,16,128]{4,3,2,1,0:T(8,128)(2,1)S(1)} %shard_map.96), channel_id=1, source_target_pairs={{0,4},{4,0},{8,12},{12,8},{16,20},{20,16},{24,28},{28,24},{32,36},... | collective-permute-start | bytes 1572872 | tf_op jit(solution)/shard_map/ppermute | solution.py:324
  92.3 0.0 copy-done.3
  92.3 0.0 copy-done.4
  92.3 0.0 copy-start.1
  92.4 2.2 %copy-done.1 = bf16[2,1024,1024]{2,1,0:T(8,128)(2,1)S(1)} copy-done((bf16[2,1024,1024]{2,1,0:T(8,128)(2,1)S(1)}, bf16[2,1024,1024]{2,1,0:T(8,128)(2,1)}, u32[]{:S(2)}) %copy-start.1) | copy-done | bytes 4194328
  94.5 2.6 %shard_map.97 = (f32[128,1024]{1,0:T(8,128)S(1)}, f32[1024,128]{1,0:T(8,128)S(1)}) custom-call(s32[1]{0:T(128)} %bitcast.half_ref, bf16[4,256,1024]{2,1,0:T(8,128)(2,1)S(1)} %all-to-all-done.1.cot_ref, bf16[16,2,4,16,128]{4,3,2,1,0:T(8,128)(2,1)S(1)} %bitcast.14, bf16[128,1024]{1,0:T(8,128)(2,1)S(1)} %bitcast.16, bf16[2,1024,1024]{2,1,0:T(8,128)(2,1)S(1)} %copy-done.1), custom_call_target="tpu_custom_call" | custom-call | flops 805306368 | bytes 3145728 | tf_op jit(solution)/shard_map/pallas_call | solution.py:221
  97.1 3.6 %collective-permute-done.1.other_ref = bf16[2,16,4,16,128]{4,3,2,1,0:T(8,128)(2,1)S(1)} collective-permute-done((bf16[2,16,4,16,128]{4,3,2,1,0:T(8,128)(2,1)S(1)}, bf16[2,16,4,16,128]{4,3,2,1,0:T(8,128)(2,1)S(1)}, u32[]{:S(2)}, u32[]{:S(2)}) %collective-permute-start.1) | collective-permute-done | bytes 524320 | tf_op jit(solution)/shard_map/ppermute | solution.py:324
  100.7 0.0 copy-done.2
  100.7 0.0 copy-done.6
  100.7 2.4 %shard_map.98 = (f32[128,1024]{1,0:T(8,128)}, f32[1024,128]{1,0:T(8,128)}, f32[1024,128]{1,0:T(8,128)}) custom-call(bf16[2,16,4,16,128]{4,3,2,1,0:T(8,128)(2,1)S(1)} %collective-permute-done.1.other_ref, f32[128,1024]{1,0:T(8,128)S(1)} %get-tuple-element.16.share_ref, f32[1024,128]{1,0:T(8,128)S(1)} %get-tuple-element.17.row_ref, ...), custom_call_target="tpu_custom_call" | custom-call | flops 268435456 | bytes 5767168 | tf_op jit(solution)/shard_map/pallas_call | solution.py:277
  (9 shorter events, 0.0 us)
Async XLA Ops:
  63.7 7.8 %copy-start.7 = (s32[1,1,2048,16]{2,3,1,0:T(8,128)S(1)}, s32[1,1,2048,16]{2,3,1,0:T(8,128)}, u32[]{:S(2)}) copy-start(s32[1,1,2048,16]{2,3,1,0:T(8,128)} %param.10) | copy-start | bytes 393220
  63.7 7.8 %copy-start.8 = (s32[1,1,2048]{2,1,0:T(1,128)S(1)}, s32[1,1,2048]{2,1,0:T(1,128)}, u32[]{:S(2)}) copy-start(s32[1,1,2048]{2,1,0:T(1,128)} %param.11) | copy-start | bytes 24580
  63.7 24.1 %all-to-all-start.1 = ((bf16[4,256,1024]{2,1,0:T(8,128)(2,1)}), bf16[4,256,1024]{2,1,0:T(8,128)(2,1)S(1)}, u32[]{:S(2)}, u32[]{:S(2)}) async-start(bf16[4,256,1024]{2,1,0:T(8,128)(2,1)} %broadcast_in_dim.15), calls=%async_computation.1 | async-start | bytes 4194304 | tf_op jit(solution)/shard_map/all_to_all | solution.py:319
  68.3 24.0 %copy-start.3 = (bf16[1,2048,128]{2,1,0:T(8,128)(2,1)S(1)}, bf16[1,2048,128]{2,1,0:T(8,128)(2,1)}, u32[]{:S(2)}) copy-start(bf16[1,2048,128]{2,1,0:T(8,128)(2,1)} %param.8) | copy-start | bytes 1572868
  68.3 24.1 %copy-start.4 = (bf16[1,128,1024]{2,1,0:T(8,128)(2,1)S(1)}, bf16[1,128,1024]{2,1,0:T(8,128)(2,1)}, u32[]{:S(2)}) copy-start(bf16[1,128,1024]{2,1,0:T(8,128)(2,1)} %param.9) | copy-start | bytes 786436
  68.3 15.8 %collective-permute-start = (bf16[2,16,4,16,128]{4,3,2,1,0:T(8,128)(2,1)}, bf16[2,16,4,16,128]{4,3,2,1,0:T(8,128)(2,1)S(1)}, u32[]{:S(2)}, u32[]{:S(2)}) collective-permute-start(bf16[2,16,4,16,128]{4,3,2,1,0:T(8,128)(2,1)} %get-tuple-element.13), channel_id=1, source_target_pairs={{0,4},{4,0},{8,12},{12,8},{16,20},{20,16},{24,28},{28,24},{32,36},... | collective-permute-start | bytes 1572872 | tf_op jit(solution)/shard_map/ppermute | solution.py:315
  82.1 2.0 %copy-start = (bf16[2,1024,1024]{2,1,0:T(8,128)(2,1)}, bf16[2,1024,1024]{2,1,0:T(8,128)(2,1)S(1)}, u32[]{:S(2)}) copy-start(bf16[2,1024,1024]{2,1,0:T(8,128)(2,1)S(1)} %get-tuple-element.15.counts_ref) | copy-start | bytes 12582916
  89.7 11.1 %collective-permute-start.1 = (bf16[2,16,4,16,128]{4,3,2,1,0:T(8,128)(2,1)S(1)}, bf16[2,16,4,16,128]{4,3,2,1,0:T(8,128)(2,1)S(1)}, u32[]{:S(2)}, u32[]{:S(2)}) collective-permute-start(bf16[2,16,4,16,128]{4,3,2,1,0:T(8,128)(2,1)S(1)} %shard_map.96), channel_id=1, source_target_pairs={{0,4},{4,0},{8,12},{12,8},{16,20},{20,16},{24,28},{28,24},{32,36},... | collective-permute-start | bytes 1572872 | tf_op jit(solution)/shard_map/ppermute | solution.py:324
  92.3 2.2 %copy-start.1 = (bf16[2,1024,1024]{2,1,0:T(8,128)(2,1)S(1)}, bf16[2,1024,1024]{2,1,0:T(8,128)(2,1)}, u32[]{:S(2)}) copy-start(bf16[2,1024,1024]{2,1,0:T(8,128)(2,1)} %copy-done) | copy-start | bytes 12582916
  94.5 6.2 %copy-start.2 = (bf16[2,1024,1024]{2,1,0:T(8,128)(2,1)S(1)}, bf16[2,1024,1024]{2,1,0:T(8,128)(2,1)}, u32[]{:S(2)}) copy-start(bf16[2,1024,1024]{2,1,0:T(8,128)(2,1)} %copy-done) | copy-start | bytes 12582916
  94.5 6.2 %copy-start.5 = (f32[1,1024,128]{2,1,0:T(8,128)S(1)}, f32[1,1024,128]{2,1,0:T(8,128)}, u32[]{:S(2)}) copy-start(f32[1,1024,128]{2,1,0:T(8,128)} %param.12) | copy-start | bytes 1572868
  94.5 6.2 %copy-start.6 = (f32[1,1024,128]{2,1,0:T(8,128)S(1)}, f32[1,1024,128]{2,1,0:T(8,128)}, u32[]{:S(2)}) copy-start(f32[1,1024,128]{2,1,0:T(8,128)} %param.13) | copy-start | bytes 1572868

commit v3 on v2

--- a/solution.py
+++ b/solution.py
@@ -38,16 +38,47 @@
     return jnp.concatenate([w[i:i + rows] for i in range(0, w.shape[0], rows)], axis=1)
 
 
-def prepare_kernel(half_ref, x_ref, pooled_ref, weight_ref, o_ref, send_ref):
+def split_kernel(x_ref, o_ref):
     towers, _, width = o_ref.shape
     for t in range(towers):
         o_ref[t] = x_ref[:, t * width:(t + 1) * width]
+
+
+def split_towers(x, towers):
+    rows, width = x.shape
+    return pl.pallas_call(
+        split_kernel,
+        out_shape=pltpu.VMEM((towers, rows, width // towers), x.dtype),
+    )(x)
+
+
+def copies_kernel(x_ref, o_ref, sems):
+    copies = [
+        pltpu.make_async_copy(x_ref, o_ref.at[i], sems.at[i]) for i in range(o_ref.shape[0])
+    ]
+    for copy in copies:
+        copy.start()
+    for copy in copies:
+        copy.wait()
+
+
+def copies_of(x, times):
+    return pl.pallas_call(
+        copies_kernel,
+        in_specs=[pl.BlockSpec(memory_space=pltpu.VMEM)],
+        out_specs=pl.BlockSpec(memory_space=pl.ANY),
+        out_shape=pltpu.HBM((times,) + x.shape, x.dtype),
+        scratch_shapes=[pltpu.SemaphoreType.DMA((times,))],
+        compiler_params=LIMIT,
+    )(pltpu.with_memory_space_constraint(x, pltpu.VMEM))
+
+
+def prepare_kernel(half_ref, pooled_ref, weight_ref, send_ref):
     send_ref[0] = pooled_ref[:, 0]
     send_ref[1] = across(weight_ref[...]).reshape(send_ref.shape[1:])
 
 
-def prepare(half, x, towers, feats, weights):
-    rows, width = x.shape
+def prepare(half, feats, weights):
     ring, halves, sides, own, emb = feats.shape
     return pl.pallas_call(
         prepare_kernel,
@@ -55,20 +86,14 @@
             num_scalar_prefetch=1,
             grid=(1,),
             in_specs=[
-                pl.BlockSpec(x.shape, lambda k, h: (0, 0)),
                 pl.BlockSpec((ring, 1, sides, own, emb), lambda k, h: (0, 1 - h[0], 0, 0, 0)),
                 pl.BlockSpec(weights.shape, lambda k, h: (0, 0)),
             ],
-            out_specs=[
-                pl.BlockSpec((towers, rows, width // towers), lambda k, h: (0, 0, 0)),
-                pl.BlockSpec((2, ring, sides, own, emb), lambda k, h: (0, 0, 0, 0, 0)),
-            ],
-        ),
-        out_shape=[
-            jax.ShapeDtypeStruct((towers, rows, width // towers), BF16),
-            jax.ShapeDtypeStruct((2, ring, sides, own, emb), BF16),
-        ],
-    )(half, x, feats, weights)
+            out_specs=pl.BlockSpec((2, ring, sides, own, emb), lambda k, h: (0, 0, 0, 0, 0)),
+        ),
+        out_shape=jax.ShapeDtypeStruct((2, ring, sides, own, emb), BF16),
+        compiler_params=LIMIT,
+    )(half, feats, weights)
 
 
 def count_kernel(half_ref, index_ref, length_ref, o_ref, done_ref):
@@ -124,7 +149,7 @@
             ],
         ),
         out_shape=[
-            jax.ShapeDtypeStruct((HALVES, rows, samples // HALVES), BF16),
+            pltpu.HBM((HALVES, rows, samples // HALVES), BF16),
             jax.ShapeDtypeStruct((8, 128), F32),
         ],
         compiler_params=LIMIT,
@@ -143,12 +168,15 @@
 def partner_kernel(cot_ref, feats_ref, weight_ref, counted_ref, o_ref, total_ref):
     del counted_ref
     k = pl.program_id(0)
-    cot = cot_ref[0]
     emb, width = total_ref.shape
     weights = along(weight_ref[0].reshape(width, emb), emb)
-    wgrad, pgrad = products(cot, feats_ref[...].reshape(cot.shape[0], emb), weights)
     ring, own = o_ref.shape[1], o_ref.shape[3]
-    o_ref[0, :, k] = pgrad.reshape(ring, own, emb)
+    blocks, rows, _ = cot_ref.shape
+    wgrad = jnp.zeros((emb, width), F32)
+    for i in range(blocks):
+        share, pgrad = products(cot_ref[i], feats_ref[0, :, i].reshape(rows, emb), weights)
+        o_ref[0, :, k * blocks + i] = pgrad.reshape(ring, own, emb)
+        wgrad += share
 
     @pl.when(k == 0)
     def _():
@@ -166,12 +194,14 @@
 def partner_part(gathered, received, counted):
     sides, rows, width = gathered.shape
     _, ring, _, own, emb = received.shape
+    steps = 2
+    blocks = sides // steps
     return pl.pallas_call(
         partner_kernel,
-        grid=(sides,),
+        grid=(steps,),
         in_specs=[
-            pl.BlockSpec((1, rows, width), lambda k: (k, 0, 0)),
-            pl.BlockSpec((1, ring, 1, own, emb), lambda k: (0, 0, k, 0, 0)),
+            pl.BlockSpec((blocks, rows, width), lambda k: (k, 0, 0)),
+            pl.BlockSpec((1, ring, blocks, own, emb), lambda k: (0, 0, k, 0, 0)),
             pl.BlockSpec((1, ring, sides, own, emb), lambda k: (1, 0, 0, 0, 0)),
             pl.BlockSpec(memory_space=pl.ANY),
         ],
@@ -249,15 +279,13 @@
 
 
 def update_kernel(
-    other_ref, share_ref, row_ref, counts_ref, slab_ref, sums_ref,
+    other_ref, part_ref, share_ref, row_ref, counts_ref, slab_ref, sums_ref,
     wgrad_ref, table_ref, fresh_ref,
 ):
     _, ring, sides, own, emb = other_ref.shape
-
-    @pl.when(pl.program_id(0) == 0)
-    def _():
-        width = share_ref.shape[1]
-        wgrad_ref[...] = share_ref[...] + along(other_ref[1].reshape(width, emb), emb).astype(F32)
+    width = share_ref.shape[1]
+    part = part_ref[0].reshape(width, emb)
+    wgrad_ref[...] = share_ref[...] + along(part, emb).astype(F32)
 
     row_grad = row_ref[...] + jnp.dot(
         counts_ref[0],
@@ -272,21 +300,22 @@
 def update(other, share, row_share, counts, slab, sums):
     _, rows, samples = counts.shape
     emb, width = share.shape
-    steps = 4
+    steps = 2
     tile = rows // steps
     return pl.pallas_call(
         update_kernel,
         grid=(steps,),
         in_specs=[
-            pl.BlockSpec(other.shape, lambda k: (0, 0, 0, 0, 0)),
-            pl.BlockSpec((emb, width), lambda k: (0, 0)),
+            pl.BlockSpec((1,) + other.shape[1:], lambda k: (0, 0, 0, 0, 0)),
+            pl.BlockSpec((1, other.shape[1] // steps) + other.shape[2:], lambda k: (1, k, 0, 0, 0)),
+            pl.BlockSpec((emb, width // steps), lambda k: (0, k)),
             pl.BlockSpec((tile, emb), lambda k: (k, 0)),
             pl.BlockSpec((1, tile, samples), lambda k: (1, k, 0)),
             pl.BlockSpec((tile, emb), lambda k: (k, 0)),
             pl.BlockSpec((tile, emb), lambda k: (k, 0)),
         ],
         out_specs=[
-            pl.BlockSpec((emb, width), lambda k: (0, 0)),
+            pl.BlockSpec((emb, width // steps), lambda k: (0, k)),
             pl.BlockSpec((tile, emb), lambda k: (k, 0)),
             pl.BlockSpec((tile, emb), lambda k: (k, 0)),
         ],
@@ -301,7 +330,7 @@
             bytes_accessed=2 * samples * rows + 16 * rows * emb + 12 * emb * width,
             transcendentals=rows * emb,
         ),
-    )(other, share, row_share, counts, slab, sums)
+    )(other, other, share, row_share, counts, slab, sums)
 
 
 def per_device(grad_inter, pooled, tower_weight, indices, lengths, table_slab, accumulator):
@@ -311,14 +340,11 @@
     weights = tower_weight[0]
     feats = pooled[0].reshape(ring_size, HALVES, sides, -1, pooled.shape[2])
 
-    parted, to_partner = prepare(half, grad_inter[0], towers, feats, weights)
-    from_partner = lax.ppermute(to_partner, PAIRED, pairs)
-    own = lax.all_to_all(parted, "tower", split_axis=0, concat_axis=0)
+    from_partner = lax.ppermute(prepare(half, feats, weights), PAIRED, pairs)
+    own = lax.all_to_all(split_towers(grad_inter[0], towers), "tower", split_axis=0, concat_axis=0)
     own = own.reshape(-1, own.shape[2])
     ring = lax.all_gather(own, RING, axis=0, tiled=True)
-    gathered = lax.all_to_all(
-        jnp.broadcast_to(ring[None], (sides,) + ring.shape), SIDE, split_axis=0, concat_axis=0
-    )
+    gathered = lax.all_to_all(copies_of(ring, sides), SIDE, split_axis=0, concat_axis=0)
     counts, counted = bag_counts(half, indices[0, 0].T, lengths[0], table_slab.shape[1])
 
     other = lax.ppermute(partner_part(gathered, from_partner, counted), PAIRED, pairs)

time: 104 us -> 101 us (0.971)
  local copies, waits for them, and re-layouts: 5.83 us -> 2.24 us
  waiting for transfers between devices: 7.3 us -> 9.61 us
    all_to_all x1, waiting for transfers between devices: 3.7 us -> 6 us  [per_device(): lax.all_to_all(copies_of(ring, sides), SIDE, split_axis=0, concat_axis=0)]
    unnamed x18 -> x16, local copies, waits for them, and re-layouts: 4.17 us -> 2.22 us
    pallas_call x1, Pallas kernels: 1.9 us -> 0.07 us  [prepare(): pl.pallas_call(prepare_kernel, grid_spec=pltpu.PrefetchScalarGridSpec(num...]
    broadcast_in_dim x1 -> x0, local copies, waits for them, and re-layouts: 1.64 us -> none  [per_device(): jnp.broadcast_to(ring[None], (sides,) + ring.shape)]
    pallas_call x2 -> x4, Pallas kernels: 4.33 us -> 5.39 us  [the longest x1 1.92 us: update(): pl.pallas_call(update_kernel, grid=(steps,), in_specs=[pl.BlockSpec((1,)...]
where the time goes in v3:
time: 101 us
  blocking collectives  59.3 us (59%)
  Pallas kernels  18.4 us (18%)
  starting transfers between devices  10.3 us (10%)
  waiting for transfers between devices  9.61 us (10%)
  local copies, waits for them, and re-layouts  2.24 us (2%)
    all_gather x1, blocking collectives, per_device(): ring = lax.all_gather(own, RING, axis=0, tiled=True)  49.7 us
    pallas_call x1, Pallas kernels, bag_counts(): pl.pallas_call(count_kernel, grid_spec=pltpu.PrefetchScalarGridSpec(num_s...  10.3 us
    all_to_all x1, blocking collectives, per_device(): lax.all_to_all(split_towers(grad_inter[0], towers), 'tower', split_axis=0...  9.53 us
    all_to_all x1, waiting for transfers between devices, per_device(): lax.all_to_all(copies_of(ring, sides), SIDE, split_axis=0, concat_axis=0)  6 us
    all_to_all x1, starting transfers between devices, per_device(): lax.all_to_all(copies_of(ring, sides), SIDE, split_axis=0, concat_axis=0)  4.61 us
    ppermute x1, waiting for transfers between devices, per_device(): lax.ppermute(partner_part(gathered, from_partner, counted), PAIRED, pairs)  3.61 us
    ppermute x1, starting transfers between devices, per_device(): from_partner = lax.ppermute(prepare(half, feats, weights), PAIRED, pairs)  3.03 us
    ppermute x1, starting transfers between devices, per_device(): lax.ppermute(partner_part(gathered, from_partner, counted), PAIRED, pairs)  2.67 us
  transfers between devices with their start and end apart: 3, of which 2 were waited for; matrix products, arithmetic and copies ran while one was open for 0% of the time, Pallas kernels for 13%

profile of v3, /device:TPU:32, one launch (start us, length us, event | category | flops | bytes accessed | tf_op | source)
XLA Modules:
  0.0 100.5 jit_solution(7985447293757870459)
XLA Ops:
  0.6 0.8 shard_map.94
  1.4 9.5 %all_to_all.10 = bf16[8,2,1024]{2,1,0:T(2,128)(2,1)S(1)} all-to-all(bf16[8,2,1024]{2,1,0:T(2,128)(2,1)S(1)} %shard_map.94), channel_id=1, replica_groups=mesh['tower'=8,'ring'=16,'half'=2,'side'=4] {'tower'}, dimensions={0} | all-to-all | bytes 65536 | tf_op jit(solution)/shard_map/all_to_all | solution.py:344
  10.9 49.7 %all_gather.3.x_ref = bf16[256,1024]{1,0:T(8,128)(2,1)S(1)} all-gather(bf16[16,1024]{1,0:T(8,128)(2,1)S(1)} %reshape.12), channel_id=1, replica_groups=mesh['tower'=8,'ring'=16,'half'=2,'side'=4] {'ring'}, dimensions={0}, use_global_device_ids=true | all-gather | bytes 557056 | tf_op jit(solution)/shard_map/all_gather | solution.py:346
  60.7 1.4 %shard_map.95 = bf16[4,256,1024]{2,1,0:T(8,128)(2,1)} custom-call(bf16[256,1024]{1,0:T(8,128)(2,1)S(1)} %all_gather.3.x_ref), custom_call_target="tpu_custom_call" | custom-call | tf_op jit(solution)/shard_map/pallas_call | solution.py:66
  62.1 0.0 copy-start.2
  62.1 0.0 copy-start.3
  62.1 0.0 copy-start.6
  62.1 0.0 copy-start.7
  62.1 4.6 %all-to-all-start.1 = ((bf16[4,256,1024]{2,1,0:T(8,128)(2,1)}), bf16[4,256,1024]{2,1,0:T(8,128)(2,1)S(1)}, u32[]{:S(2)}, u32[]{:S(2)}) async-start(bf16[4,256,1024]{2,1,0:T(8,128)(2,1)} %shard_map.95), calls=%async_computation.1 | async-start | bytes 4194304 | tf_op jit(solution)/shard_map/all_to_all | solution.py:347
  66.7 0.1 shard_map.96
  66.8 3.0 %collective-permute-start = (bf16[2,16,4,16,128]{4,3,2,1,0:T(8,128)(2,1)S(1)}, bf16[2,16,4,16,128]{4,3,2,1,0:T(8,128)(2,1)S(1)}, u32[]{:S(2)}, u32[]{:S(2)}) collective-permute-start(bf16[2,16,4,16,128]{4,3,2,1,0:T(8,128)(2,1)S(1)} %shard_map.96), channel_id=1, source_target_pairs={{0,4},{4,0},{8,12},{12,8},{16,20},{20,16},{24,28},{28,24},{32,36},... | collective-permute-start | bytes 1572872 | tf_op jit(solution)/shard_map/ppermute | solution.py:343
  69.8 0.0 copy-done.6
  69.9 0.0 copy-done.7
  69.9 10.3 %shard_map.97 = (bf16[2,1024,1024]{2,1,0:T(8,128)(2,1)}, f32[8,128]{1,0:T(8,128)S(1)}) custom-call(s32[1]{0:T(128)} %bitcast.1.half_ref, s32[16,2048]{1,0:T(8,128)S(1)} %bitcast.19, s32[1,2048]{1,0:T(1,128)S(1)} %bitcast.20), custom_call_target="tpu_custom_call" | custom-call | flops 100663296 | bytes 4194304 | tf_op jit(solution)/shard_map/pallas_call | solution.py:137
  80.2 0.0 collective-permute-done.feats_ref.weight_ref
  80.2 6.0 %all-to-all-done.1.cot_ref = bf16[4,256,1024]{2,1,0:T(8,128)(2,1)S(1)} async-done(((bf16[4,256,1024]{2,1,0:T(8,128)(2,1)}), bf16[4,256,1024]{2,1,0:T(8,128)(2,1)S(1)}, u32[]{:S(2)}, u32[]{:S(2)}) %all-to-all-start.1) | async-done | bytes 2097184 | tf_op jit(solution)/shard_map/all_to_all | solution.py:347
  86.2 1.3 %shard_map.98 = bf16[2,16,4,16,128]{4,3,2,1,0:T(8,128)(2,1)S(1)} custom-call(bf16[4,256,1024]{2,1,0:T(8,128)(2,1)S(1)} %all-to-all-done.1.cot_ref, bf16[2,16,4,16,128]{4,3,2,1,0:T(8,128)(2,1)S(1)} %collective-permute-done.feats_ref.weight_ref, bf16[2,16,4,16,128]{4,3,2,1,0:T(8,128)(2,1)S(1)} %collective-permute-done.feats_ref.weight_ref, ...), custom_call_target="tpu_custom_call" | custom-call | flops 536870912 | bytes 3145728 | tf_op jit(solution)/shard_map/pallas_call | solution.py:199
  87.5 2.7 %collective-permute-start.1 = (bf16[2,16,4,16,128]{4,3,2,1,0:T(8,128)(2,1)S(1)}, bf16[2,16,4,16,128]{4,3,2,1,0:T(8,128)(2,1)S(1)}, u32[]{:S(2)}, u32[]{:S(2)}) collective-permute-start(bf16[2,16,4,16,128]{4,3,2,1,0:T(8,128)(2,1)S(1)} %shard_map.98), channel_id=1, source_target_pairs={{0,4},{4,0},{8,12},{12,8},{16,20},{20,16},{24,28},{28,24},{32,36},... | collective-permute-start | bytes 1572872 | tf_op jit(solution)/shard_map/ppermute | solution.py:350
  90.2 0.0 copy-start
  90.2 2.2 %copy-done = bf16[2,1024,1024]{2,1,0:T(8,128)(2,1)S(1)} copy-done((bf16[2,1024,1024]{2,1,0:T(8,128)(2,1)S(1)}, bf16[2,1024,1024]{2,1,0:T(8,128)(2,1)}, u32[]{:S(2)}) %copy-start) | copy-done | bytes 4194328
  92.4 2.6 %shard_map.99 = (f32[128,1024]{1,0:T(8,128)S(1)}, f32[1024,128]{1,0:T(8,128)S(1)}) custom-call(s32[1]{0:T(128)} %bitcast.1.half_ref, bf16[4,256,1024]{2,1,0:T(8,128)(2,1)S(1)} %all-to-all-done.1.cot_ref, bf16[16,2,4,16,128]{4,3,2,1,0:T(8,128)(2,1)S(1)} %bitcast.14, bf16[128,1024]{1,0:T(8,128)(2,1)S(1)} %bitcast.16, bf16[2,1024,1024]{2,1,0:T(8,128)(2,1)S(1)} %copy-done), custom_call_target="tpu_custom_call" | custom-call | flops 805306368 | bytes 3145728 | tf_op jit(solution)/shard_map/pallas_call | solution.py:251
  95.0 3.6 %collective-permute-done.1.other_ref.part_ref = bf16[2,16,4,16,128]{4,3,2,1,0:T(8,128)(2,1)S(1)} collective-permute-done((bf16[2,16,4,16,128]{4,3,2,1,0:T(8,128)(2,1)S(1)}, bf16[2,16,4,16,128]{4,3,2,1,0:T(8,128)(2,1)S(1)}, u32[]{:S(2)}, u32[]{:S(2)}) %collective-permute-start.1) | collective-permute-done | bytes 524320 | tf_op jit(solution)/shard_map/ppermute | solution.py:350
  98.6 0.0 copy-done.4
  98.6 1.9 %shard_map.100 = (f32[128,1024]{1,0:T(8,128)}, f32[1024,128]{1,0:T(8,128)}, f32[1024,128]{1,0:T(8,128)}) custom-call(bf16[2,16,4,16,128]{4,3,2,1,0:T(8,128)(2,1)S(1)} %collective-permute-done.1.other_ref.part_ref, bf16[2,16,4,16,128]{4,3,2,1,0:T(8,128)(2,1)S(1)} %collective-permute-done.1.other_ref.part_ref, f32[128,1024]{1,0:T(8,128)S(1)} %get-tuple-element.12.share_ref, ...), custom_call_target="tpu_custom_call" | custom-call | flops 268435456 | bytes 5767168 | tf_op jit(solution)/shard_map/pallas_call | solution.py:305
  (8 shorter events, 0.0 us)
Async XLA Ops:
  62.1 4.7 %copy-start.2 = (bf16[1,2048,128]{2,1,0:T(8,128)(2,1)S(1)}, bf16[1,2048,128]{2,1,0:T(8,128)(2,1)}, u32[]{:S(2)}) copy-start(bf16[1,2048,128]{2,1,0:T(8,128)(2,1)} %param.8) | copy-start | bytes 1572868
  62.1 4.6 %copy-start.3 = (bf16[1,128,1024]{2,1,0:T(8,128)(2,1)S(1)}, bf16[1,128,1024]{2,1,0:T(8,128)(2,1)}, u32[]{:S(2)}) copy-start(bf16[1,128,1024]{2,1,0:T(8,128)(2,1)} %param.9) | copy-start | bytes 786436
  62.1 7.8 %copy-start.6 = (s32[1,1,2048,16]{2,3,1,0:T(8,128)S(1)}, s32[1,1,2048,16]{2,3,1,0:T(8,128)}, u32[]{:S(2)}) copy-start(s32[1,1,2048,16]{2,3,1,0:T(8,128)} %param.10) | copy-start | bytes 393220
  62.1 7.7 %copy-start.7 = (s32[1,1,2048]{2,1,0:T(1,128)S(1)}, s32[1,1,2048]{2,1,0:T(1,128)}, u32[]{:S(2)}) copy-start(s32[1,1,2048]{2,1,0:T(1,128)} %param.11) | copy-start | bytes 24580
  62.1 24.1 %all-to-all-start.1 = ((bf16[4,256,1024]{2,1,0:T(8,128)(2,1)}), bf16[4,256,1024]{2,1,0:T(8,128)(2,1)S(1)}, u32[]{:S(2)}, u32[]{:S(2)}) async-start(bf16[4,256,1024]{2,1,0:T(8,128)(2,1)} %shard_map.95), calls=%async_computation.1 | async-start | bytes 4194304 | tf_op jit(solution)/shard_map/all_to_all | solution.py:347
  66.8 13.4 %collective-permute-start = (bf16[2,16,4,16,128]{4,3,2,1,0:T(8,128)(2,1)S(1)}, bf16[2,16,4,16,128]{4,3,2,1,0:T(8,128)(2,1)S(1)}, u32[]{:S(2)}, u32[]{:S(2)}) collective-permute-start(bf16[2,16,4,16,128]{4,3,2,1,0:T(8,128)(2,1)S(1)} %shard_map.96), channel_id=1, source_target_pairs={{0,4},{4,0},{8,12},{12,8},{16,20},{20,16},{24,28},{28,24},{32,36},... | collective-permute-start | bytes 1572872 | tf_op jit(solution)/shard_map/ppermute | solution.py:343
  87.5 11.1 %collective-permute-start.1 = (bf16[2,16,4,16,128]{4,3,2,1,0:T(8,128)(2,1)S(1)}, bf16[2,16,4,16,128]{4,3,2,1,0:T(8,128)(2,1)S(1)}, u32[]{:S(2)}, u32[]{:S(2)}) collective-permute-start(bf16[2,16,4,16,128]{4,3,2,1,0:T(8,128)(2,1)S(1)} %shard_map.98), channel_id=1, source_target_pairs={{0,4},{4,0},{8,12},{12,8},{16,20},{20,16},{24,28},{28,24},{32,36},... | collective-permute-start | bytes 1572872 | tf_op jit(solution)/shard_map/ppermute | solution.py:350
  90.2 2.2 %copy-start = (bf16[2,1024,1024]{2,1,0:T(8,128)(2,1)S(1)}, bf16[2,1024,1024]{2,1,0:T(8,128)(2,1)}, u32[]{:S(2)}) copy-start(bf16[2,1024,1024]{2,1,0:T(8,128)(2,1)} %get-tuple-element.11.counts_ref) | copy-start | bytes 12582916
  92.4 6.2 %copy-start.1 = (bf16[2,1024,1024]{2,1,0:T(8,128)(2,1)S(1)}, bf16[2,1024,1024]{2,1,0:T(8,128)(2,1)}, u32[]{:S(2)}) copy-start(bf16[2,1024,1024]{2,1,0:T(8,128)(2,1)} %get-tuple-element.11.counts_ref) | copy-start | bytes 12582916
  92.4 6.2 %copy-start.4 = (f32[1,1024,128]{2,1,0:T(8,128)S(1)}, f32[1,1024,128]{2,1,0:T(8,128)}, u32[]{:S(2)}) copy-start(f32[1,1024,128]{2,1,0:T(8,128)} %param.12) | copy-start | bytes 1572868
  92.4 6.2 %copy-start.5 = (f32[1,1024,128]{2,1,0:T(8,128)S(1)}, f32[1,1024,128]{2,1,0:T(8,128)}, u32[]{:S(2)}) copy-start(f32[1,1024,128]{2,1,0:T(8,128)} %param.13) | copy-start | bytes 1572868

commit v4 on v3

--- a/solution.py
+++ b/solution.py
@@ -165,56 +165,42 @@
     return wgrad, pgrad.astype(BF16)
 
 
-def partner_kernel(cot_ref, feats_ref, weight_ref, counted_ref, o_ref, total_ref):
+def partner_kernel(cot_ref, received_ref, counted_ref, o_ref):
     del counted_ref
-    k = pl.program_id(0)
-    emb, width = total_ref.shape
-    weights = along(weight_ref[0].reshape(width, emb), emb)
-    ring, own = o_ref.shape[1], o_ref.shape[3]
-    blocks, rows, _ = cot_ref.shape
+    _, ring, sides, own, emb = o_ref.shape
+    _, rows, width = cot_ref.shape
+    weights = along(received_ref[1].reshape(width, emb), emb)
     wgrad = jnp.zeros((emb, width), F32)
-    for i in range(blocks):
-        share, pgrad = products(cot_ref[i], feats_ref[0, :, i].reshape(rows, emb), weights)
-        o_ref[0, :, k * blocks + i] = pgrad.reshape(ring, own, emb)
+    for k in range(sides):
+        share, pgrad = products(cot_ref[k], received_ref[0, :, k].reshape(rows, emb), weights)
+        o_ref[0, :, k] = pgrad.reshape(ring, own, emb)
         wgrad += share
-
-    @pl.when(k == 0)
-    def _():
-        total_ref[...] = wgrad
-
-    @pl.when(k > 0)
-    def _():
-        total_ref[...] += wgrad
-
-    @pl.when(k == pl.num_programs(0) - 1)
-    def _():
-        o_ref[1] = across(total_ref[...].astype(BF16)).reshape(o_ref.shape[1:])
+    o_ref[1] = across(wgrad.astype(BF16)).reshape(o_ref.shape[1:])
 
 
 def partner_part(gathered, received, counted):
     sides, rows, width = gathered.shape
-    _, ring, _, own, emb = received.shape
-    steps = 2
-    blocks = sides // steps
+    emb = received.shape[-1]
     return pl.pallas_call(
         partner_kernel,
-        grid=(steps,),
         in_specs=[
-            pl.BlockSpec((blocks, rows, width), lambda k: (k, 0, 0)),
-            pl.BlockSpec((1, ring, blocks, own, emb), lambda k: (0, 0, k, 0, 0)),
-            pl.BlockSpec((1, ring, sides, own, emb), lambda k: (1, 0, 0, 0, 0)),
+            pl.BlockSpec(memory_space=pltpu.VMEM),
+            pl.BlockSpec(memory_space=pltpu.VMEM),
             pl.BlockSpec(memory_space=pl.ANY),
         ],
-        out_specs=pl.BlockSpec(received.shape, lambda k: (0, 0, 0, 0, 0)),
+        out_specs=pl.BlockSpec(memory_space=pltpu.VMEM),
         out_shape=jax.ShapeDtypeStruct(received.shape, BF16),
-        scratch_shapes=[pltpu.VMEM((emb, width), F32)],
         compiler_params=LIMIT,
         cost_estimate=pl.CostEstimate(
             flops=4 * sides * rows * emb * width,
             bytes_accessed=2 * sides * rows * width + 4 * received.size,
             transcendentals=0,
         ),
-    )(gathered, received, received, counted)
+    )(
+        pltpu.with_memory_space_constraint(gathered, pltpu.VMEM),
+        pltpu.with_memory_space_constraint(received, pltpu.VMEM),
+        counted,
+    )
 
 
 def own_kernel(
@@ -279,22 +265,26 @@
 
 
 def update_kernel(
-    other_ref, part_ref, share_ref, row_ref, counts_ref, slab_ref, sums_ref,
+    other_ref, share_ref, row_ref, counts_ref, slab_ref, sums_ref,
     wgrad_ref, table_ref, fresh_ref,
 ):
     _, ring, sides, own, emb = other_ref.shape
-    width = share_ref.shape[1]
-    part = part_ref[0].reshape(width, emb)
-    wgrad_ref[...] = share_ref[...] + along(part, emb).astype(F32)
-
-    row_grad = row_ref[...] + jnp.dot(
-        counts_ref[0],
+    step = pl.program_id(0)
+    width = wgrad_ref.shape[1]
+    tile = table_ref.shape[0]
+    tiles = ring * width // share_ref.shape[1]
+    part = other_ref[1, pl.ds(step * tiles, tiles)].reshape(width, emb)
+    columns = pl.ds(pl.multiple_of(step * width, width), width)
+    wgrad_ref[...] = share_ref[:, columns] + along(part, emb).astype(F32)
+    rows = pl.ds(pl.multiple_of(step * tile, tile), tile)
+    row_grad = row_ref[rows, :] + jnp.dot(
+        counts_ref[1, rows, :],
         other_ref[0].reshape(ring * sides * own, emb),
         preferred_element_type=F32,
     )
-    fresh = sums_ref[...] + row_grad * row_grad
+    fresh = sums_ref[rows, :] + row_grad * row_grad
     fresh_ref[...] = fresh
-    table_ref[...] = slab_ref[...] - learn_rate * row_grad / (jnp.sqrt(fresh) + epsilon)
+    table_ref[...] = slab_ref[rows, :] - learn_rate * row_grad / (jnp.sqrt(fresh) + epsilon)
 
 
 def update(other, share, row_share, counts, slab, sums):
@@ -302,18 +292,14 @@
     emb, width = share.shape
     steps = 2
     tile = rows // steps
+    near = [
+        pltpu.with_memory_space_constraint(x, pltpu.VMEM)
+        for x in (other, share, row_share, counts, slab, sums)
+    ]
     return pl.pallas_call(
         update_kernel,
         grid=(steps,),
-        in_specs=[
-            pl.BlockSpec((1,) + other.shape[1:], lambda k: (0, 0, 0, 0, 0)),
-            pl.BlockSpec((1, other.shape[1] // steps) + other.shape[2:], lambda k: (1, k, 0, 0, 0)),
-            pl.BlockSpec((emb, width // steps), lambda k: (0, k)),
-            pl.BlockSpec((tile, emb), lambda k: (k, 0)),
-            pl.BlockSpec((1, tile, samples), lambda k: (1, k, 0)),
-            pl.BlockSpec((tile, emb), lambda k: (k, 0)),
-            pl.BlockSpec((tile, emb), lambda k: (k, 0)),
-        ],
+        in_specs=[pl.BlockSpec(memory_space=pltpu.VMEM)] * len(near),
         out_specs=[
             pl.BlockSpec((emb, width // steps), lambda k: (0, k)),
             pl.BlockSpec((tile, emb), lambda k: (k, 0)),
@@ -330,7 +316,7 @@
             bytes_accessed=2 * samples * rows + 16 * rows * emb + 12 * emb * width,
             transcendentals=rows * emb,
         ),
-    )(other, other, share, row_share, counts, slab, sums)
+    )(*near)
 
 
 def per_device(grad_inter, pooled, tower_weight, indices, lengths, table_slab, accumulator):

time: 101 us -> 101 us (level)
  no operation moved by 1% of the time
where the time goes in v4:
time: 101 us; the launch traced here: 100 us
  blocking collectives  59.3 us (59%)
  Pallas kernels  18 us (18%)
  starting transfers between devices  10.3 us (10%)
  waiting for transfers between devices  9.62 us (10%)
  local copies, waits for them, and re-layouts  2.24 us (2%)
    all_gather x1, blocking collectives, per_device(): ring = lax.all_gather(own, RING, axis=0, tiled=True)  49.7 us
    pallas_call x1, Pallas kernels, bag_counts(): pl.pallas_call(count_kernel, grid_spec=pltpu.PrefetchScalarGridSpec(num_s...  10.3 us
    all_to_all x1, blocking collectives, per_device(): lax.all_to_all(split_towers(grad_inter[0], towers), 'tower', split_axis=0...  9.53 us
    all_to_all x1, waiting for transfers between devices, per_device(): lax.all_to_all(copies_of(ring, sides), SIDE, split_axis=0, concat_axis=0)  6 us
    all_to_all x1, starting transfers between devices, per_device(): lax.all_to_all(copies_of(ring, sides), SIDE, split_axis=0, concat_axis=0)  4.61 us
    ppermute x1, waiting for transfers between devices, per_device(): lax.ppermute(partner_part(gathered, from_partner, counted), PAIRED, pairs)  3.61 us
    ppermute x1, starting transfers between devices, per_device(): from_partner = lax.ppermute(prepare(half, feats, weights), PAIRED, pairs)  3.03 us
    ppermute x1, starting transfers between devices, per_device(): lax.ppermute(partner_part(gathered, from_partner, counted), PAIRED, pairs)  2.67 us
  transfers between devices with their start and end apart: 3, of which 2 were waited for; matrix products, arithmetic and copies ran while one was open for 0% of the time, Pallas kernels for 13%

profile of v4, /device:TPU:32, one launch (start us, length us, event | category | flops | bytes accessed | tf_op | source)
XLA Modules:
  0.0 100.2 jit_solution(1153627137824463311)
XLA Ops:
  0.6 0.8 shard_map.94
  1.4 9.5 %all_to_all.10 = bf16[8,2,1024]{2,1,0:T(2,128)(2,1)S(1)} all-to-all(bf16[8,2,1024]{2,1,0:T(2,128)(2,1)S(1)} %shard_map.94), channel_id=1, replica_groups=mesh['tower'=8,'ring'=16,'half'=2,'side'=4] {'tower'}, dimensions={0} | all-to-all | bytes 65536 | tf_op jit(solution)/shard_map/all_to_all | solution.py:330
  10.9 49.7 %all_gather.3.x_ref = bf16[256,1024]{1,0:T(8,128)(2,1)S(1)} all-gather(bf16[16,1024]{1,0:T(8,128)(2,1)S(1)} %reshape.12), channel_id=1, replica_groups=mesh['tower'=8,'ring'=16,'half'=2,'side'=4] {'ring'}, dimensions={0}, use_global_device_ids=true | all-gather | bytes 557056 | tf_op jit(solution)/shard_map/all_gather | solution.py:332
  60.7 1.4 %shard_map.95 = bf16[4,256,1024]{2,1,0:T(8,128)(2,1)} custom-call(bf16[256,1024]{1,0:T(8,128)(2,1)S(1)} %all_gather.3.x_ref), custom_call_target="tpu_custom_call" | custom-call | tf_op jit(solution)/shard_map/pallas_call | solution.py:66
  62.1 0.0 copy-start.2
  62.1 0.0 copy-start.3
  62.1 0.0 copy-start.6
  62.1 0.0 copy-start.7
  62.1 4.6 %all-to-all-start.1 = ((bf16[4,256,1024]{2,1,0:T(8,128)(2,1)}), bf16[4,256,1024]{2,1,0:T(8,128)(2,1)S(1)}, u32[]{:S(2)}, u32[]{:S(2)}) async-start(bf16[4,256,1024]{2,1,0:T(8,128)(2,1)} %shard_map.95), calls=%async_computation.1 | async-start | bytes 4194304 | tf_op jit(solution)/shard_map/all_to_all | solution.py:333
  66.7 0.0 copy-done.2
  66.7 0.0 copy-done.3
  66.7 0.1 shard_map.96
  66.8 3.0 %collective-permute-start = (bf16[2,16,4,16,128]{4,3,2,1,0:T(8,128)(2,1)S(1)}, bf16[2,16,4,16,128]{4,3,2,1,0:T(8,128)(2,1)S(1)}, u32[]{:S(2)}, u32[]{:S(2)}) collective-permute-start(bf16[2,16,4,16,128]{4,3,2,1,0:T(8,128)(2,1)S(1)} %shard_map.96), channel_id=1, source_target_pairs={{0,4},{4,0},{8,12},{12,8},{16,20},{20,16},{24,28},{28,24},{32,36},... | collective-permute-start | bytes 1572872 | tf_op jit(solution)/shard_map/ppermute | solution.py:329
  69.8 0.0 copy-done.6
  69.9 10.3 %shard_map.97 = (bf16[2,1024,1024]{2,1,0:T(8,128)(2,1)}, f32[8,128]{1,0:T(8,128)S(1)}) custom-call(s32[1]{0:T(128)} %bitcast.1.half_ref, s32[16,2048]{1,0:T(8,128)S(1)} %bitcast.19, s32[1,2048]{1,0:T(1,128)S(1)} %bitcast.20), custom_call_target="tpu_custom_call" | custom-call | flops 100663296 | bytes 4194304 | tf_op jit(solution)/shard_map/pallas_call | solution.py:137
  80.2 0.0 collective-permute-done.received_ref
  80.2 6.0 %all-to-all-done.1.cot_ref = bf16[4,256,1024]{2,1,0:T(8,128)(2,1)S(1)} async-done(((bf16[4,256,1024]{2,1,0:T(8,128)(2,1)}), bf16[4,256,1024]{2,1,0:T(8,128)(2,1)S(1)}, u32[]{:S(2)}, u32[]{:S(2)}) %all-to-all-start.1) | async-done | bytes 2097184 | tf_op jit(solution)/shard_map/all_to_all | solution.py:333
  86.2 1.0 %shard_map.98 = bf16[2,16,4,16,128]{4,3,2,1,0:T(8,128)(2,1)S(1)} custom-call(bf16[4,256,1024]{2,1,0:T(8,128)(2,1)S(1)} %all-to-all-done.1.cot_ref, bf16[2,16,4,16,128]{4,3,2,1,0:T(8,128)(2,1)S(1)} %collective-permute-done.received_ref, f32[8,128]{1,0:T(8,128)S(1)} %get-tuple-element.10.counted_ref), custom_call_target="tpu_custom_call" | custom-call | flops 536870912 | bytes 3145728 | tf_op jit(solution)/shard_map/pallas_call | solution.py:184
  87.2 2.7 %collective-permute-start.1 = (bf16[2,16,4,16,128]{4,3,2,1,0:T(8,128)(2,1)S(1)}, bf16[2,16,4,16,128]{4,3,2,1,0:T(8,128)(2,1)S(1)}, u32[]{:S(2)}, u32[]{:S(2)}) collective-permute-start(bf16[2,16,4,16,128]{4,3,2,1,0:T(8,128)(2,1)S(1)} %shard_map.98), channel_id=1, source_target_pairs={{0,4},{4,0},{8,12},{12,8},{16,20},{20,16},{24,28},{28,24},{32,36},... | collective-permute-start | bytes 1572872 | tf_op jit(solution)/shard_map/ppermute | solution.py:336
  89.9 2.2 %copy-done = bf16[2,1024,1024]{2,1,0:T(8,128)(2,1)S(1)} copy-done((bf16[2,1024,1024]{2,1,0:T(8,128)(2,1)S(1)}, bf16[2,1024,1024]{2,1,0:T(8,128)(2,1)}, u32[]{:S(2)}) %copy-start) | copy-done | bytes 4194328
  92.1 2.6 %shard_map.99 = (f32[128,1024]{1,0:T(8,128)S(1)}, f32[1024,128]{1,0:T(8,128)S(1)}) custom-call(s32[1]{0:T(128)} %bitcast.1.half_ref, bf16[4,256,1024]{2,1,0:T(8,128)(2,1)S(1)} %all-to-all-done.1.cot_ref, bf16[16,2,4,16,128]{4,3,2,1,0:T(8,128)(2,1)S(1)} %bitcast.14, bf16[128,1024]{1,0:T(8,128)(2,1)S(1)} %bitcast.16, bf16[2,1024,1024]{2,1,0:T(8,128)(2,1)S(1)} %copy-done), custom_call_target="tpu_custom_call" | custom-call | flops 805306368 | bytes 3145728 | tf_op jit(solution)/shard_map/pallas_call | solution.py:237
  94.7 3.6 %collective-permute-done.1.other_ref = bf16[2,16,4,16,128]{4,3,2,1,0:T(8,128)(2,1)S(1)} collective-permute-done((bf16[2,16,4,16,128]{4,3,2,1,0:T(8,128)(2,1)S(1)}, bf16[2,16,4,16,128]{4,3,2,1,0:T(8,128)(2,1)S(1)}, u32[]{:S(2)}, u32[]{:S(2)}) %collective-permute-start.1) | collective-permute-done | bytes 524320 | tf_op jit(solution)/shard_map/ppermute | solution.py:336
  98.3 0.0 copy-done.1
  98.3 1.9 %shard_map.100 = (f32[128,1024]{1,0:T(8,128)}, f32[1024,128]{1,0:T(8,128)}, f32[1024,128]{1,0:T(8,128)}) custom-call(bf16[2,16,4,16,128]{4,3,2,1,0:T(8,128)(2,1)S(1)} %collective-permute-done.1.other_ref, f32[128,1024]{1,0:T(8,128)S(1)} %get-tuple-element.12.share_ref, f32[1024,128]{1,0:T(8,128)S(1)} %get-tuple-element.13.row_ref, ...), custom_call_target="tpu_custom_call" | custom-call | flops 268435456 | bytes 5767168 | tf_op jit(solution)/shard_map/pallas_call | solution.py:299
  (8 shorter events, 0.0 us)
Async XLA Ops:
  62.1 4.7 %copy-start.2 = (bf16[1,2048,128]{2,1,0:T(8,128)(2,1)S(1)}, bf16[1,2048,128]{2,1,0:T(8,128)(2,1)}, u32[]{:S(2)}) copy-start(bf16[1,2048,128]{2,1,0:T(8,128)(2,1)} %param.8) | copy-start | bytes 1572868
  62.1 4.6 %copy-start.3 = (bf16[1,128,1024]{2,1,0:T(8,128)(2,1)S(1)}, bf16[1,128,1024]{2,1,0:T(8,128)(2,1)}, u32[]{:S(2)}) copy-start(bf16[1,128,1024]{2,1,0:T(8,128)(2,1)} %param.9) | copy-start | bytes 786436
  62.1 7.8 %copy-start.6 = (s32[1,1,2048,16]{2,3,1,0:T(8,128)S(1)}, s32[1,1,2048,16]{2,3,1,0:T(8,128)}, u32[]{:S(2)}) copy-start(s32[1,1,2048,16]{2,3,1,0:T(8,128)} %param.10) | copy-start | bytes 393220
  62.1 7.7 %copy-start.7 = (s32[1,1,2048]{2,1,0:T(1,128)S(1)}, s32[1,1,2048]{2,1,0:T(1,128)}, u32[]{:S(2)}) copy-start(s32[1,1,2048]{2,1,0:T(1,128)} %param.11) | copy-start | bytes 24580
  62.1 24.1 %all-to-all-start.1 = ((bf16[4,256,1024]{2,1,0:T(8,128)(2,1)}), bf16[4,256,1024]{2,1,0:T(8,128)(2,1)S(1)}, u32[]{:S(2)}, u32[]{:S(2)}) async-start(bf16[4,256,1024]{2,1,0:T(8,128)(2,1)} %shard_map.95), calls=%async_computation.1 | async-start | bytes 4194304 | tf_op jit(solution)/shard_map/all_to_all | solution.py:333
  66.8 13.4 %collective-permute-start = (bf16[2,16,4,16,128]{4,3,2,1,0:T(8,128)(2,1)S(1)}, bf16[2,16,4,16,128]{4,3,2,1,0:T(8,128)(2,1)S(1)}, u32[]{:S(2)}, u32[]{:S(2)}) collective-permute-start(bf16[2,16,4,16,128]{4,3,2,1,0:T(8,128)(2,1)S(1)} %shard_map.96), channel_id=1, source_target_pairs={{0,4},{4,0},{8,12},{12,8},{16,20},{20,16},{24,28},{28,24},{32,36},... | collective-permute-start | bytes 1572872 | tf_op jit(solution)/shard_map/ppermute | solution.py:329
  87.2 11.1 %collective-permute-start.1 = (bf16[2,16,4,16,128]{4,3,2,1,0:T(8,128)(2,1)S(1)}, bf16[2,16,4,16,128]{4,3,2,1,0:T(8,128)(2,1)S(1)}, u32[]{:S(2)}, u32[]{:S(2)}) collective-permute-start(bf16[2,16,4,16,128]{4,3,2,1,0:T(8,128)(2,1)S(1)} %shard_map.98), channel_id=1, source_target_pairs={{0,4},{4,0},{8,12},{12,8},{16,20},{20,16},{24,28},{28,24},{32,36},... | collective-permute-start | bytes 1572872 | tf_op jit(solution)/shard_map/ppermute | solution.py:336
  89.9 2.2 %copy-start = (bf16[2,1024,1024]{2,1,0:T(8,128)(2,1)S(1)}, bf16[2,1024,1024]{2,1,0:T(8,128)(2,1)}, u32[]{:S(2)}) copy-start(bf16[2,1024,1024]{2,1,0:T(8,128)(2,1)} %get-tuple-element.11.counts_ref) | copy-start | bytes 12582916
  92.1 6.2 %copy-start.1 = (bf16[2,1024,1024]{2,1,0:T(8,128)(2,1)S(1)}, bf16[2,1024,1024]{2,1,0:T(8,128)(2,1)}, u32[]{:S(2)}) copy-start(bf16[2,1024,1024]{2,1,0:T(8,128)(2,1)} %get-tuple-element.11.counts_ref) | copy-start | bytes 12582916
  92.1 6.2 %copy-start.4 = (f32[1,1024,128]{2,1,0:T(8,128)S(1)}, f32[1,1024,128]{2,1,0:T(8,128)}, u32[]{:S(2)}) copy-start(f32[1,1024,128]{2,1,0:T(8,128)} %param.12) | copy-start | bytes 1572868
  92.1 6.2 %copy-start.5 = (f32[1,1024,128]{2,1,0:T(8,128)S(1)}, f32[1,1024,128]{2,1,0:T(8,128)}, u32[]{:S(2)}) copy-start(f32[1,1024,128]{2,1,0:T(8,128)} %param.13) | copy-start | bytes 1572868
